TPU v7x, 32 devices: a whole 2x2x4 slice. The times are simulated.
32 devices in a mesh: dp: 8 (over y, x, core), section: 4 (over z).
Axes of the slice: x: 2, y: 2, z: 4, core: 2. Of those that a mesh axis runs over, the one named last changes fastest.
Arguments:
- inputs: bfloat16 [16, 128, 768], P('dp', 'section'), may hold values from -6 to 6
- other_view: bfloat16 [16, 256, 768], P('dp', 'section'), may hold values from -6 to 6
- mats: bfloat16 [4, 2, 768, 3072], P('section'), may hold values from -24 to 24
- vectors: float32 [4, 7, 768], P('section'), may hold values from -2 to 2
- mixing: float32 [16], P('dp'), may hold values from 0.2 to 0.8
- partner: int32 [16], P('dp'), may hold values from 0 to 1
- segments: int32 [16, 128], P('dp'), may hold values from 0 to 2, never falling along the last dimension, each value on 1 to 64 neighbouring positions
- cotangent: bfloat16 [16, 128, 768], P('dp'), may hold values from -6 to 6
Outputs:
- activations: bfloat16 [4, 16, 128, 768], P('section', 'dp')
- input_grad: bfloat16 [16, 128, 768], P('dp', 'section')
- view_grad: bfloat16 [16, 256, 768], P('dp', 'section')
- mats_grad: float32 [4, 2, 768, 3072], P('section')
- vectors_grad: float32 [4, 7, 768], P('section')
Inputs may be any that keep to these rules, and one draw needn't show every extreme that they name: `segments`: clip numbers never fall along a row; each clip has 1 to 64 tokens and one has exactly that many.
All inputs are finite; a program needn't handle non-finite values.
Results may differ from a plain program's by a relative error of at most 0.018.
Values may be sent and summed in bfloat16 or wider, within the bound.
A program may use at most 192 MiB of HBM per device.

v0:
```python
from functools import partial

import jax
import jax.numpy as jnp
from jax import lax
from jax.sharding import PartitionSpec as P

D = 768
HEAD = 64


def shifted(block, axis, distance):
    devices = range(lax.axis_size(axis))
    route = [((i - distance) % len(devices), i) for i in devices]
    return lax.ppermute(block, axis, route)


def shifted_2(value, axis, steps):
    count = lax.axis_size(axis)
    initial, last = (max(0, -steps), min(count, count - steps))
    return lax.ppermute(value, axis, [(source, source + steps) for source in range(initial, last)])


def layer_norm(stream, norm_gain, norm_shift):
    center = stream - jnp.mean(stream, axis=-1, keepdims=True)
    spread = jnp.mean(center * center, axis=-1, keepdims=True)
    return center * lax.rsqrt(spread + 1e-06) * norm_gain + norm_shift


def matmul(multiplier, multiplicand):
    return jnp.dot(multiplier, multiplicand, preferred_element_type=jnp.float32)


def times_transposed(multiplier, multiplicand):
    return lax.dot_general(
        multiplier, multiplicand, (((1,), (1,)), ((), ())), preferred_element_type=jnp.float32
    )


def transposed_times(multiplier, multiplicand):
    return lax.dot_general(
        multiplier, multiplicand, (((0,), (0,)), ((), ())), preferred_element_type=jnp.float32
    )


def split_heads(states):
    return states.reshape(states.shape[0], -1, HEAD)


def masked_scores(queries, key_states, query_ids, key_ids):
    scores = jnp.einsum(
        "qhd,khd->hqk",
        split_heads(queries),
        split_heads(key_states),
        preferred_element_type=jnp.float32,
    )
    allowed = (query_ids[:, None] == key_ids[None, :])[None]
    return jnp.where(allowed, scores * HEAD ** (-0.5), -1000000000.0)


def attention_forward(queries, key_states, value_states, query_ids, key_ids):
    scores = masked_scores(queries, key_states, query_ids, key_ids)
    row_max = jnp.max(scores, axis=-1, keepdims=True)
    weights = jnp.exp(scores - row_max)
    row_total = jnp.sum(weights, axis=-1, keepdims=True)
    weights = (weights / row_total).astype(jnp.bfloat16)
    attended = jnp.einsum(
        "hqk,khd->qhd", weights, split_heads(value_states), preferred_element_type=jnp.float32
    )
    return (
        attended.reshape(queries.shape[0], -1).astype(jnp.bfloat16),
        row_max + jnp.log(row_total),
    )


def attention_backward(
    queries, key_states, value_states, query_ids, key_ids, log_total, grad_attended
):
    scores = masked_scores(queries, key_states, query_ids, key_ids)
    weights = jnp.exp(scores - log_total)
    grad_split = split_heads(grad_attended)
    grad_weights = jnp.einsum(
        "qhd,khd->hqk", grad_split, split_heads(value_states), preferred_element_type=jnp.float32
    )
    weighted_sum = jnp.sum(weights * grad_weights, axis=-1, keepdims=True)
    grad_scores = (weights * (grad_weights - weighted_sum)).astype(jnp.bfloat16)
    scale_factor = HEAD ** (-0.5)
    grad_q = (
        jnp.einsum(
            "hqk,khd->qhd", grad_scores, split_heads(key_states), preferred_element_type=jnp.float32
        )
        * scale_factor
    )
    grad_k = (
        jnp.einsum(
            "hqk,qhd->khd", grad_scores, split_heads(queries), preferred_element_type=jnp.float32
        )
        * scale_factor
    )
    grad_v = jnp.einsum(
        "hqk,qhd->khd", weights.astype(jnp.bfloat16), grad_split, preferred_element_type=jnp.float32
    )
    query_count = queries.shape[0]
    key_count = key_states.shape[0]
    return (
        grad_q.reshape(query_count, -1),
        grad_k.reshape(key_count, -1),
        grad_v.reshape(key_count, -1),
    )


def self_forward(stream, query_ids, first, vector):
    normed = layer_norm(stream, vector[0], vector[1]).astype(jnp.bfloat16)
    projected = matmul(normed, first[:, : 3 * D])
    queries = (projected[:, :D] + vector[5]).astype(jnp.bfloat16)
    key_states = projected[:, D : 2 * D].astype(jnp.bfloat16)
    value_states = (projected[:, 2 * D :] + vector[2]).astype(jnp.bfloat16)
    attended, total = attention_forward(queries, key_states, value_states, query_ids, query_ids)
    output = stream + matmul(attended, first[:, 3 * D :]) + vector[4]
    return (output, (normed, queries, key_states, value_states, attended, total))


def self_output(stream, source, query_ids, first, second, vector):
    return self_forward(stream, query_ids, first, vector)[0]


def self_backward(
    stream, source, query_ids, first, second, vector, incoming, grad_mats, grad_vector
):
    normed, queries, key_states, value_states, attended, total = self_forward(
        stream, query_ids, first, vector
    )[1]
    rounded_out = incoming.astype(jnp.bfloat16)
    grad_out = transposed_times(attended, rounded_out)
    grad_attended = times_transposed(rounded_out, first[:, 3 * D :]).astype(jnp.bfloat16)
    grad_q, grad_k, grad_v = attention_backward(
        queries, key_states, value_states, query_ids, query_ids, total, grad_attended
    )
    grad_projected = jnp.concatenate([grad_q, grad_k, grad_v], axis=1).astype(jnp.bfloat16)
    grad_in = transposed_times(normed, grad_projected)
    grad_normed = times_transposed(grad_projected, first[:, : 3 * D])
    grad_stream_norm, grad_gain, grad_shift = jax.vjp(layer_norm, stream, vector[0], vector[1])[1](
        grad_normed
    )
    empty_row = jnp.zeros(vector[0].shape, jnp.float32)
    grad_first = jnp.concatenate([grad_in, grad_out], axis=1)
    grad_bias = jnp.stack(
        [
            grad_gain,
            grad_shift,
            jnp.sum(grad_projected[:, 2 * D :], axis=0, dtype=jnp.float32),
            empty_row,
            jnp.sum(incoming, axis=0),
            jnp.sum(grad_projected[:, :D], axis=0, dtype=jnp.float32),
            empty_row,
        ]
    )
    return (
        incoming + grad_stream_norm,
        jnp.zeros(source.shape, jnp.float32),
        grad_mats + jnp.stack([grad_first, jnp.zeros(second.shape, jnp.float32)]),
        grad_vector + grad_bias,
    )


def merging_forward(stream, source, query_ids, first, second, vector):
    source_ids = jnp.repeat(query_ids, 2)
    normed_cross = layer_norm(stream, vector[0], vector[1]).astype(jnp.bfloat16)
    queries = matmul(normed_cross, first[:, :D]).astype(jnp.bfloat16)
    projected = matmul(source, first[:, D : 3 * D]).astype(jnp.bfloat16)
    attended_cross, total_cross = attention_forward(
        queries, projected[:, :D], projected[:, D:], query_ids, source_ids
    )
    middle = stream + matmul(attended_cross, first[:, 3 * D :]) + vector[4]
    normed_self = layer_norm(middle, vector[2], vector[3]).astype(jnp.bfloat16)
    projected_self = matmul(normed_self, second[:, : 3 * D])
    queries_self = (projected_self[:, :D] + vector[5]).astype(jnp.bfloat16)
    others_self = projected_self[:, D:].astype(jnp.bfloat16)
    attended_self, total_self = attention_forward(
        queries_self, others_self[:, :D], others_self[:, D:], query_ids, query_ids
    )
    output = middle + matmul(attended_self, second[:, 3 * D :]) + vector[6]
    kept = (
        source_ids,
        normed_cross,
        queries,
        projected,
        attended_cross,
        total_cross,
        middle,
        normed_self,
        queries_self,
        others_self,
        attended_self,
        total_self,
    )
    return (output, kept)


def merging_output(stream, source, query_ids, first, second, vector):
    return merging_forward(stream, source, query_ids, first, second, vector)[0]


def merging_backward(
    stream, source, query_ids, first, second, vector, incoming, grad_mats, grad_vector
):
    kept = merging_forward(stream, source, query_ids, first, second, vector)[1]
    source_ids, normed_cross, queries, projected, attended_cross, total_cross = kept[:6]
    middle, normed_self, queries_self, others_self, attended_self, total_self = kept[6:]
    rounded_out = incoming.astype(jnp.bfloat16)
    grad_out_self = transposed_times(attended_self, rounded_out)
    grad_attended = times_transposed(rounded_out, second[:, 3 * D :]).astype(jnp.bfloat16)
    grad_q, grad_k, grad_v = attention_backward(
        queries_self,
        others_self[:, :D],
        others_self[:, D:],
        query_ids,
        query_ids,
        total_self,
        grad_attended,
    )
    grad_projected = jnp.concatenate([grad_q, grad_k, grad_v], axis=1).astype(jnp.bfloat16)
    grad_in_self = transposed_times(normed_self, grad_projected)
    grad_normed = times_transposed(grad_projected, second[:, : 3 * D])
    grad_middle_norm, grad_gain_self, grad_shift_self = jax.vjp(
        layer_norm, middle, vector[2], vector[3]
    )[1](grad_normed)
    grad_middle = incoming + grad_middle_norm
    rounded_middle = grad_middle.astype(jnp.bfloat16)
    grad_out_cross = transposed_times(attended_cross, rounded_middle)
    grad_attended = times_transposed(rounded_middle, first[:, 3 * D :]).astype(jnp.bfloat16)
    grad_q, grad_k, grad_v = attention_backward(
        queries,
        projected[:, :D],
        projected[:, D:],
        query_ids,
        source_ids,
        total_cross,
        grad_attended,
    )
    grad_query = grad_q.astype(jnp.bfloat16)
    grad_pair = jnp.concatenate([grad_k, grad_v], axis=1).astype(jnp.bfloat16)
    grad_source = times_transposed(grad_pair, first[:, D : 3 * D])
    grad_normed = times_transposed(grad_query, first[:, :D])
    grad_stream_norm, grad_gain_cross, grad_shift_cross = jax.vjp(
        layer_norm, stream, vector[0], vector[1]
    )[1](grad_normed)
    grad_first = jnp.concatenate(
        [
            transposed_times(normed_cross, grad_query),
            transposed_times(source, grad_pair),
            grad_out_cross,
        ],
        axis=1,
    )
    grad_second = jnp.concatenate([grad_in_self, grad_out_self], axis=1)
    grad_bias = jnp.stack(
        [
            grad_gain_cross,
            grad_shift_cross,
            grad_gain_self,
            grad_shift_self,
            jnp.sum(grad_middle, axis=0),
            jnp.sum(grad_projected[:, :D], axis=0, dtype=jnp.float32),
            jnp.sum(incoming, axis=0),
        ]
    )
    return (
        grad_middle + grad_stream_norm,
        grad_source,
        grad_mats + jnp.stack([grad_first, grad_second]),
        grad_vector + grad_bias,
    )


def forward_mlp(stream, first, second, vector):
    normed = layer_norm(stream, vector[0], vector[1]).astype(jnp.bfloat16)
    hidden = matmul(normed, first) + vector[2:6].reshape(-1)
    active = jax.nn.gelu(hidden, approximate=False).astype(jnp.bfloat16)
    return (stream + times_transposed(active, second) + vector[6], (normed, hidden, active))


def mlp_output(stream, source, query_ids, first, second, vector):
    return forward_mlp(stream, first, second, vector)[0]


def backward_mlp(
    stream, source, query_ids, first, second, vector, incoming, grad_mats, grad_vector
):
    normed, hidden, active = forward_mlp(stream, first, second, vector)[1]
    rounded_out = incoming.astype(jnp.bfloat16)
    grad_second = transposed_times(rounded_out, active)
    grad_active = matmul(rounded_out, second)
    grad_hidden = jax.vjp(partial(jax.nn.gelu, approximate=False), hidden)[1](grad_active)[
        0
    ].astype(jnp.bfloat16)
    grad_first = transposed_times(normed, grad_hidden)
    grad_normed = times_transposed(grad_hidden, first)
    grad_stream_norm, grad_gain, grad_shift = jax.vjp(layer_norm, stream, vector[0], vector[1])[1](
        grad_normed
    )
    hidden_bias = jnp.sum(grad_hidden, axis=0, dtype=jnp.float32).reshape(4, -1)
    grad_bias = jnp.concatenate(
        [grad_gain[None], grad_shift[None], hidden_bias, jnp.sum(incoming, axis=0)[None]], axis=0
    )
    return (
        incoming + grad_stream_norm,
        jnp.zeros(source.shape, jnp.float32),
        grad_mats + jnp.stack([grad_first, grad_second]),
        grad_vector + grad_bias,
    )


def spare_output(stream, source, query_ids, first, second, vector):
    return jnp.zeros(stream.shape, jnp.float32)


def spare_backward(
    stream, source, query_ids, first, second, vector, incoming, grad_mats, grad_vector
):
    return (
        jnp.zeros(stream.shape, jnp.float32),
        jnp.zeros(source.shape, jnp.float32),
        grad_mats,
        grad_vector,
    )


def blend(own_rows, far_rows, mixing, partner):
    chosen = jnp.take(far_rows, partner, axis=0).astype(jnp.float32)
    share = mixing[:, None, None]
    return share * own_rows.astype(jnp.float32) + (1.0 - share) * chosen


def on_device(inputs, other_view, mats, vectors, mixing, partner, segments, cotangent):
    sections = lax.axis_size("section")
    place = lax.axis_index("section")
    batch = mixing.shape[0]
    half_away = lax.axis_size("dp") // 2
    row_tokens = segments.shape[1]
    whole_inputs, whole_view = (
        lax.all_gather(inputs, "section", axis=1, tiled=True),
        lax.all_gather(other_view, "section", axis=1, tiled=True),
    )
    joined_whole = jnp.concatenate([whole_inputs, whole_view], axis=1)
    far_whole = shifted(joined_whole, "dp", half_away)
    blended = blend(joined_whole, far_whole, mixing, partner)
    stream_all = blended[:, :row_tokens]
    view_all = blended[:, row_tokens:]
    source_all = view_all.astype(jnp.bfloat16)
    first = mats[0, 0]
    second = mats[0, 1]
    vector = vectors[0]
    kind = jnp.where(place % 2 == 1, 3, jnp.where(place == 0, 1, 2))
    steps_total = sections + batch - 1
    received = jnp.zeros((row_tokens, D), jnp.bfloat16)
    kept_inputs = jnp.zeros((batch, row_tokens, D), jnp.float32)
    records = jnp.zeros((batch, row_tokens, D), jnp.bfloat16)
    for clock in range(steps_total):
        index = clock - place
        valid = (index >= 0) & (index < batch)
        safe = jnp.clip(index, 0, batch - 1)
        entry = jnp.where(place == 0, stream_all[safe], received.astype(jnp.float32))
        output = lax.switch(
            jnp.where(valid, kind, 0),
            [spare_output, self_output, merging_output, mlp_output],
            entry,
            source_all[safe],
            segments[safe],
            first,
            second,
            vector,
        )
        sent = output.astype(jnp.bfloat16)
        kept_inputs = kept_inputs.at[safe].set(jnp.where(valid, entry, kept_inputs[safe]))
        records = records.at[safe].set(jnp.where(valid, sent, records[safe]))
        if clock + 1 < steps_total:
            received = shifted_2(sent, "section", 1)
    last_section = sections - 1
    grad_received = jnp.zeros((row_tokens, D), jnp.bfloat16)
    grad_inputs = jnp.zeros((batch, row_tokens, D), jnp.float32)
    grad_sources = jnp.zeros(source_all.shape, jnp.float32)
    grad_mats = jnp.zeros((2,) + first.shape, jnp.float32)
    grad_vector = jnp.zeros(vector.shape, jnp.float32)
    for clock in range(steps_total):
        index = clock - (last_section - place)
        valid = (index >= 0) & (index < batch)
        safe = jnp.clip(index, 0, batch - 1)
        incoming = jnp.where(
            place == last_section,
            cotangent[safe].astype(jnp.float32),
            grad_received.astype(jnp.float32),
        )
        grad_stream, grad_source, grad_mats, grad_vector = lax.switch(
            jnp.where(valid, kind, 0),
            [spare_backward, self_backward, merging_backward, backward_mlp],
            kept_inputs[safe],
            source_all[safe],
            segments[safe],
            first,
            second,
            vector,
            incoming,
            grad_mats,
            grad_vector,
        )
        grad_inputs = grad_inputs.at[safe].set(
            jnp.where(valid & (place == 0), grad_stream, grad_inputs[safe])
        )
        grad_sources = grad_sources.at[safe].add(grad_source)
        if clock + 1 < steps_total:
            grad_received = shifted_2(grad_stream.astype(jnp.bfloat16), "section", -1)
    summed_mats, summed_vector = lax.psum((grad_mats, grad_vector), "dp")
    part_inputs, part_view = (
        lax.psum_scatter(
            grad_inputs.astype(jnp.bfloat16), "section", scatter_dimension=1, tiled=True
        ).astype(jnp.float32),
        lax.psum_scatter(
            grad_sources.astype(jnp.bfloat16), "section", scatter_dimension=1, tiled=True
        ).astype(jnp.float32),
    )
    joined_grads = jnp.concatenate([part_inputs, part_view], axis=1)
    owed = (1.0 - mixing)[:, None, None] * joined_grads
    picked = (partner[:, None] == jnp.arange(batch, dtype=jnp.int32)[None, :]).astype(jnp.float32)
    sent_back = jnp.sum(picked[:, :, None, None] * owed[:, None], axis=0).astype(jnp.bfloat16)
    arrived = shifted(sent_back, "dp", half_away).astype(jnp.float32)
    combined = mixing[:, None, None] * joined_grads + arrived
    quarter = part_inputs.shape[1]
    return (
        records[None],
        combined[:, :quarter].astype(jnp.bfloat16),
        combined[:, quarter:].astype(jnp.bfloat16),
        summed_mats[None],
        summed_vector[None],
    )


def solution(mesh):
    in_specs = (
        P("dp", "section", None),
        P("dp", "section", None),
        P("section", None, None, None),
        P("section", None, None),
        P("dp"),
        P("dp"),
        P("dp", None),
        P("dp", None, None),
    )
    out_specs = (
        P("section", "dp", None, None),
        P("dp", "section", None),
        P("dp", "section", None),
        P("section", None, None, None),
        P("section", None, None),
    )
    return jax.shard_map(
        on_device, mesh=mesh, in_specs=in_specs, out_specs=out_specs, check_vma=False
    )
```

profile of v0, /device:TPU:9, one launch (start us, length us, event | category | flops | bytes accessed | tf_op | source)
XLA Modules:
  0.0 817.3 jit_solution(17764964340984023710)
XLA Ops:
  8.0 12.0 %all_gather.6 = bf16[2,128,768]{2,1,0:T(8,128)(2,1)S(1)} all-gather(bf16[2,32,768]{2,1,0:T(8,128)(2,1)} %param.88), channel_id=1, replica_groups=mesh['dp'=8,'section'=4] {'section'}, dimensions={1}, use_global_device_ids=true | all-gather | bytes 491520 | tf_op jit(solution)/shard_map/all_gather | solution.py:342
  20.1 15.7 %all_gather.7 = bf16[2,256,768]{2,1,0:T(8,128)(2,1)S(1)} all-gather(bf16[2,64,768]{2,1,0:T(8,128)(2,1)} %param.89), channel_id=1, replica_groups=mesh['dp'=8,'section'=4] {'section'}, dimensions={1}, use_global_device_ids=true | all-gather | bytes 983040 | tf_op jit(solution)/shard_map/all_gather | solution.py:343
  38.8 8.4 %slice_bitcast_fusion = (bf16[768,3072]{1,0:T(8,128)(2,1)}, bf16[768,3072]{1,0:T(8,128)(2,1)}) fusion(bf16[1,2,768,3072]{3,2,1,0:T(8,128)(2,1)} %param.90), kind=kLoop, calls=%fused_computation.2004 | loop fusion | bytes 18874368 | tf_op jit(solution)/shard_map/squeeze | solution.py:352
  47.1 11.0 %collective-permute-done = bf16[2,384,768]{2,1,0:T(8,128)(2,1)} collective-permute-done((bf16[2,384,768]{2,1,0:T(8,128)(2,1)S(1)}, bf16[2,384,768]{2,1,0:T(8,128)(2,1)}, u32[]{:S(2)}, u32[]{:S(2)}) %collective-permute-start) | collective-permute-done | bytes 1179680 | tf_op jit(solution)/shard_map/ppermute | solution.py:15
  61.6 6.5 conditional.10
  68.2 1.9 collective-permute-start.1
  70.3 12.2 %collective-permute-done.1 = bf16[128,768]{1,0:T(8,128)(2,1)S(1)} collective-permute-done((bf16[128,768]{1,0:T(8,128)(2,1)S(1)}, bf16[128,768]{1,0:T(8,128)(2,1)S(1)}, u32[]{:S(2)}, u32[]{:S(2)}) %collective-permute-start.1) | collective-permute-done | bytes 196640 | tf_op jit(solution)/shard_map/ppermute | solution.py:21
  84.2 10.3 %conditional.11 = (bf16[128,768]{1,0:T(8,128)(2,1)S(1)}) conditional(s32[]{:T(128)} %clamp.31, () %tuple.288, (f32[128,768]{1,0:T(8,128)S(1)}, f32[7,768]{1,0:T(8,128)S(1)}, bf16[768,3072]{1,0:T(8,128)(2,1)}, s32[1,128]{1,0:T(1,128)S(1)}) %tuple.715, (bf16[2,256,768]{2,1,0:T(8,128)(2,1)S(1)}, s32[]{:T(128)}, ...), branch_computations={%region_20.21_spmd, %region_21.26_spmd, %region_26.35_spmd, %regio... | conditional | flops 1693731072 | bytes 45478060 | solution.py:364
  84.8 9.4 %fusion.213 = bf16[128,768]{1,0:T(8,128)(2,1)S(1)} fusion(f32[128,768]{1,0:T(8,128)S(1)} %get-tuple-element.930, bf16[768,3072]{1,0:T(8,128)(2,1)} %get-tuple-element.933, bf16[768,3072]{1,0:T(8,128)(2,1)} %get-tuple-element.932, f32[3072]{0:T(1024)S(1)} %add.1751, f32[768]{0:T(1024)S(1)} %get-tuple-element.1174, f32[768]{0:T(1024)S(1)} %get-tuple-element.1175, ...), kind=kOutput, calls=%fused_computation.314 | convolution fusion | flops 1234698240 | bytes 10049536 | tf_op jit(solution)/shard_map/cond/branch_3_fun/dot_general | solution.py:35
  94.5 1.9 collective-permute-start.2
  97.9 7.3 collective-permute-done.2
  106.9 10.7 %conditional.12 = (bf16[128,768]{1,0:T(8,128)(2,1)S(1)}) conditional(s32[]{:T(128)} %clamp.32, () %tuple.292, (f32[128,768]{1,0:T(8,128)S(1)}, f32[7,768]{1,0:T(8,128)S(1)}, bf16[768,3072]{1,0:T(8,128)(2,1)}, s32[1,128]{1,0:T(1,128)S(1)}) %tuple.718, (bf16[2,256,768]{2,1,0:T(8,128)(2,1)S(1)}, s32[]{:T(128)}, ...), branch_computations={%region_39.40_spmd, %region_40.45_spmd, %region_45.54_spmd, %regio... | conditional | flops 1693731072 | bytes 45465744 | solution.py:364
  107.6 9.4 %fusion.355 = bf16[128,768]{1,0:T(8,128)(2,1)S(1)} fusion(f32[128,768]{1,0:T(8,128)S(1)} %get-tuple-element.945, bf16[768,3072]{1,0:T(8,128)(2,1)} %get-tuple-element.948, bf16[768,3072]{1,0:T(8,128)(2,1)} %get-tuple-element.947, f32[3072]{0:T(1024)S(1)} %add.1795, f32[768]{0:T(1024)S(1)} %get-tuple-element.1189, f32[768]{0:T(1024)S(1)} %get-tuple-element.1190, ...), kind=kOutput, calls=%fused_computation.507 | convolution fusion | flops 1234698240 | bytes 10049536 | tf_op jit(solution)/shard_map/cond/branch_3_fun/dot_general | solution.py:35
  117.6 13.1 %collective-permute-start.3 = (bf16[128,768]{1,0:T(8,128)(2,1)S(1)}, bf16[128,768]{1,0:T(8,128)(2,1)S(1)}, u32[]{:S(2)}, u32[]{:S(2)}) collective-permute-start(bf16[128,768]{1,0:T(8,128)(2,1)S(1)} %get-tuple-element.1754), channel_id=1, source_target_pairs={{0,1},{1,2},{2,3},{4,5},{5,6},{6,7},{8,9},{9,10},{10,11},{12,13},{... | collective-permute-start | bytes 589832 | tf_op jit(solution)/shard_map/ppermute | solution.py:21
  133.9 7.5 conditional.13
  141.5 27.3 %collective-permute-start.4 = (bf16[128,768]{1,0:T(8,128)(2,1)S(1)}, bf16[128,768]{1,0:T(8,128)(2,1)S(1)}, u32[]{:S(2)}, u32[]{:S(2)}) collective-permute-start(bf16[128,768]{1,0:T(8,128)(2,1)S(1)} %get-tuple-element.1755), channel_id=1, source_target_pairs={{0,1},{1,2},{2,3},{4,5},{5,6},{6,7},{8,9},{9,10},{10,11},{12,13},{... | collective-permute-start | bytes 589832 | tf_op jit(solution)/shard_map/ppermute | solution.py:21
  171.4 2.4 fusion.1197
  174.8 17.3 %conditional.15 = (f32[128,768]{1,0:T(8,128)}, f32[256,768]{1,0:T(8,128)}, f32[2,768,3072]{2,1,0:T(8,128)}, f32[7,768]{1,0:T(8,128)S(1)}) conditional(s32[]{:T(128)} %clamp.35, () %tuple.304, (f32[128,768]{1,0:T(8,128)S(1)}, f32[7,768]{1,0:T(8,128)S(1)}, bf16[768,3072]{1,0:T(8,128)(2,1)}, s32[1,128]{1,0:T(1,128)S(1)}, ...), branch_computations={%region_96.97_spmd, %region_97.110_spmd, %region_110.132_spmd, %re... | conditional | flops 4870117376 | bytes 218971264 | solution.py:394
  176.6 9.2 %broadcast_in_dim.764 = f32[2,768,3072]{2,1,0:T(8,128)} broadcast(f32[]{:T(128)} %constant.1418.clone), dimensions={} | broadcast | bytes 18874372 | tf_op jit(solution)/shard_map/broadcast_in_dim | solution.py:383
  193.2 1.9 collective-permute-start.5
  197.7 2.4 collective-permute-done.5
  200.2 9.1 %conditional.16 = (f32[128,768]{1,0:T(8,128)}, f32[2,768,3072]{2,1,0:T(8,128)}, f32[7,768]{1,0:T(8,128)S(1)}, f32[1,256,768]{2,1,0:T(8,128)}) conditional(s32[]{:T(128)} %clamp.36, (f32[2,768,3072]{2,1,0:T(8,128)}, f32[7,768]{1,0:T(8,128)S(1)}) %tuple.308, (f32[128,768]{1,0:T(8,128)S(1)}, f32[7,768]{1,0:T(8,128)S(1)}, ...), branch_computations={%region_142.143_spmd, %region_143.156_spmd, %region_156.178_spmd, ... | conditional | flops 4874841088 | bytes 227623744 | solution.py:394
  210.4 1.9 collective-permute-start.6
  212.3 2.5 fusion.1196
  216.6 2.0 fusion.1187
  218.7 96.7 %collective-permute-done.6 = bf16[128,768]{1,0:T(8,128)(2,1)S(1)} collective-permute-done((bf16[128,768]{1,0:T(8,128)(2,1)S(1)}, bf16[128,768]{1,0:T(8,128)(2,1)S(1)}, u32[]{:S(2)}, u32[]{:S(2)}) %collective-permute-start.6) | collective-permute-done | bytes 196640 | tf_op jit(solution)/shard_map/ppermute | solution.py:21
  315.4 44.5 %conditional.17 = (f32[128,768]{1,0:T(8,128)}, f32[2,768,3072]{2,1,0:T(8,128)}, f32[7,768]{1,0:T(8,128)S(1)}, f32[1,256,768]{2,1,0:T(8,128)}) conditional(s32[]{:T(128)} %clamp.37, (f32[2,768,3072]{2,1,0:T(8,128)}, f32[7,768]{1,0:T(8,128)S(1)}) %tuple.312, (f32[128,768]{1,0:T(8,128)S(1)}, f32[7,768]{1,0:T(8,128)S(1)}, ...), branch_computations={%region_188.189_spmd, %region_189.202_spmd, %region_202.224_spmd, ... | conditional | flops 4874841088 | bytes 224477952 | solution.py:394
  325.1 3.4 convolution_add_fusion.30
  328.5 6.8 convert_reduce_fusion.11
  338.2 3.9 convolution_bitcast_fusion.4
  343.6 15.0 %maximum_add_fusion.4 = f32[2,768,3072]{2,1,0:T(8,128)} fusion(f32[2,768,3072]{2,1,0:T(8,128)} %get-tuple-element.1047, f32[1,768,3072]{2,1,0:T(8,128)S(1)} %convolution_bitcast_fusion.4, f32[1,768,3072]{2,1,0:T(8,128)S(1)} %convolution_bitcast_fusion.5), kind=kLoop, calls=%fused_computation.1547 | loop fusion | flops 9437184 | bytes 56623104 | tf_op jit(solution)/shard_map/cond/branch_3_fun/add | solution.py:309
  363.0 2.4 fusion.1195
  367.2 48.9 %collective-permute-done.7 = bf16[128,768]{1,0:T(8,128)(2,1)S(1)} collective-permute-done((bf16[128,768]{1,0:T(8,128)(2,1)S(1)}, bf16[128,768]{1,0:T(8,128)(2,1)S(1)}, u32[]{:S(2)}, u32[]{:S(2)}) %collective-permute-start.7) | collective-permute-done | bytes 196640 | tf_op jit(solution)/shard_map/ppermute | solution.py:21
  416.1 44.3 %conditional.18 = (f32[128,768]{1,0:T(8,128)}, f32[2,768,3072]{2,1,0:T(8,128)}, f32[7,768]{1,0:T(8,128)S(1)}, f32[1,256,768]{2,1,0:T(8,128)}) conditional(s32[]{:T(128)} %clamp.38, (f32[2,768,3072]{2,1,0:T(8,128)}, f32[7,768]{1,0:T(8,128)S(1)}) %tuple.316, (f32[128,768]{1,0:T(8,128)S(1)}, f32[7,768]{1,0:T(8,128)S(1)}, ...), branch_computations={%region_234.235_spmd, %region_235.248_spmd, %region_248.270_spmd, ... | conditional | flops 4874841088 | bytes 224477952 | solution.py:394
  425.8 3.3 convolution_add_fusion.32
  429.1 6.8 convert_reduce_fusion.15
  438.9 3.9 convolution_bitcast_fusion.6
  444.3 15.0 %maximum_add_fusion.7 = f32[2,768,3072]{2,1,0:T(8,128)} fusion(f32[2,768,3072]{2,1,0:T(8,128)} %get-tuple-element.1073, f32[1,768,3072]{2,1,0:T(8,128)S(1)} %convolution_bitcast_fusion.6, f32[1,768,3072]{2,1,0:T(8,128)S(1)} %convolution_bitcast_fusion.7), kind=kLoop, calls=%fused_computation.1755 | loop fusion | flops 9437184 | bytes 56623104 | tf_op jit(solution)/shard_map/cond/branch_3_fun/add | solution.py:309
  461.5 1.9 collective-permute-start.8
  463.5 2.5 fusion.1194
  468.0 10.4 %conditional.19 = (f32[128,768]{1,0:T(8,128)}, f32[2,768,3072]{2,1,0:T(8,128)}, f32[7,768]{1,0:T(8,128)S(1)}, f32[1,256,768]{2,1,0:T(8,128)}) conditional(s32[]{:T(128)} %clamp.39, (f32[2,768,3072]{2,1,0:T(8,128)}, f32[7,768]{1,0:T(8,128)S(1)}) %tuple.320, (f32[128,768]{1,0:T(8,128)S(1)}, f32[7,768]{1,0:T(8,128)S(1)}, ...), branch_computations={%region_280.281_spmd, %region_281.294_spmd, %region_294.316_spmd, ... | conditional | flops 4874841088 | bytes 224477952 | solution.py:394
  478.4 2.5 fusion.1193
  484.8 1.9 fusion.1189
  492.9 63.2 %reduce-scatter.3.cloned.1.call-done = bf16[2,32,768]{2,1,0:T(8,128)(2,1)} async-done(((bf16[2,128,768]{2,1,0:T(8,128)(2,1)}), bf16[2,32,768]{2,1,0:T(8,128)(2,1)}) %reduce-scatter.3.cloned.1.call-update) | async-done | bytes 98320 | tf_op jit(solution)/shard_map/reduce_scatter | solution.py:415
  556.1 26.0 %reduce-scatter.5.cloned.1.call-done = bf16[2,64,768]{2,1,0:T(8,128)(2,1)} async-done(((bf16[2,256,768]{2,1,0:T(8,128)(2,1)}), bf16[2,64,768]{2,1,0:T(8,128)(2,1)}) %reduce-scatter.5.cloned.1.call-update) | async-done | bytes 196624 | tf_op jit(solution)/shard_map/reduce_scatter | solution.py:418
  589.8 22.1 %psum.15 = f32[1,7,768]{2,0,1:T(1,128)} all-reduce(f32[1,7,768]{2,0,1:T(1,128)S(1)} %broadcast_in_dim.863), channel_id=1, replica_groups=mesh['dp'=8,'section'=4] {'dp'}, use_global_device_ids=true, to_apply=%region_329.330 | all-reduce | flops 5376 | bytes 43008 | tf_op jit(solution)/shard_map/psum | solution.py:413
  614.6 182.2 %all-reduce.7.cloned.1.call-done = f32[1,2,768,3072]{3,2,1,0:T(8,128)} async-done(((f32[1,2,768,3072]{3,2,1,0:T(8,128)}), f32[1,2,768,3072]{3,2,1,0:T(8,128)}) %all-reduce.7.cloned.1.call-update) | async-done | bytes 18874384 | tf_op jit(solution)/shard_map/psum | solution.py:413
  796.7 12.9 %copy.813 = f32[1,2,768,3072]{3,2,1,0:T(8,128)} copy(f32[1,2,768,3072]{3,2,1,0:T(8,128)} %all-reduce.7.cloned.1.call-done) | data formatting | bytes 37748736
  (231 shorter events, 70.2 us)
Async XLA Ops:
  8.0 548.1 %reduce-scatter.3.cloned.1.call-start = ((), (), s32[]{:S(2)}) async-start(), calls=%async_computation.2 | async-start | bytes 491520 | tf_op jit(solution)/shard_map/reduce_scatter | solution.py:415
  20.0 17.1 %copy-start.204 = (s32[2]{0:T(128)S(1)}, s32[2]{0:T(128)}, u32[]{:S(2)}) copy-start(s32[2]{0:T(128)} %param.93) | copy-start | bytes 28
  20.0 17.2 %copy-start.198 = (f32[2]{0:T(128)S(1)}, f32[2]{0:T(128)}, u32[]{:S(2)}) copy-start(f32[2]{0:T(128)} %param.92) | copy-start | bytes 28
  20.0 17.3 %copy-start.172 = (s32[2,128]{1,0:T(2,128)S(1)}, s32[2,128]{1,0:T(2,128)}, u32[]{:S(2)}) copy-start(s32[2,128]{1,0:T(2,128)} %param.94) | copy-start | bytes 3076
  20.0 17.9 %copy-start.178 = (f32[1,7,768]{2,0,1:T(1,128)S(1)}, f32[1,7,768]{2,0,1:T(1,128)}, u32[]{:S(2)}) copy-start(f32[1,7,768]{2,0,1:T(1,128)} %param.91) | copy-start | bytes 64516
  20.1 17.9 %copy-start.189 = (s32[3]{0:T(128)S(1)}, s32[3]{0:T(128)}, u32[]{:S(2)}) copy-start(s32[3]{0:T(128)} %constant.1673.clone.1) | copy-start | bytes 40
  35.9 22.3 %collective-permute-start = (bf16[2,384,768]{2,1,0:T(8,128)(2,1)S(1)}, bf16[2,384,768]{2,1,0:T(8,128)(2,1)}, u32[]{:S(2)}, u32[]{:S(2)}) collective-permute-start(bf16[2,384,768]{2,1,0:T(8,128)(2,1)S(1)} %constant_dynamic-update-slice_fusion), channel_id=1, source_target_pairs={{16,0},{20,4},{24,8},{28,12},{0,16},{4,20},{8,24},{12,28},{17,1},{... | collective-permute-start | bytes 3538952 | tf_op jit(solution)/shard_map/ppermute | solution.py:15
  37.2 22.9 %copy-start.200 = (f32[2]{0:T(128)}, f32[2]{0:T(128)S(1)}, u32[]{:S(2)}) copy-start(f32[2]{0:T(128)S(1)} %broadcast_subtract_fusion) | copy-start | bytes 28
  60.8 114.1 %copy-start.26 = (bf16[2,256,768]{2,1,0:T(8,128)(2,1)}, bf16[2,256,768]{2,1,0:T(8,128)(2,1)S(1)}, u32[]{:S(2)}) copy-start(bf16[2,256,768]{2,1,0:T(8,128)(2,1)S(1)} %slice.2184) | copy-start | bytes 2359300
  68.2 16.0 %copy-start.129 = (bf16[128,768]{1,0:T(8,128)(2,1)}, bf16[128,768]{1,0:T(8,128)(2,1)S(1)}, u32[]{:S(2)}) copy-start(bf16[128,768]{1,0:T(8,128)(2,1)S(1)} %get-tuple-element.1752) | copy-start | bytes 589828
  68.2 14.3 %collective-permute-start.1 = (bf16[128,768]{1,0:T(8,128)(2,1)S(1)}, bf16[128,768]{1,0:T(8,128)(2,1)S(1)}, u32[]{:S(2)}, u32[]{:S(2)}) collective-permute-start(bf16[128,768]{1,0:T(8,128)(2,1)S(1)} %get-tuple-element.1752), channel_id=1, source_target_pairs={{0,1},{1,2},{2,3},{4,5},{5,6},{6,7},{8,9},{9,10},{10,11},{12,13},{... | collective-permute-start | bytes 589832 | tf_op jit(solution)/shard_map/ppermute | solution.py:21
  94.5 12.4 %copy-start.131 = (bf16[128,768]{1,0:T(8,128)(2,1)}, bf16[128,768]{1,0:T(8,128)(2,1)S(1)}, u32[]{:S(2)}) copy-start(bf16[128,768]{1,0:T(8,128)(2,1)S(1)} %get-tuple-element.1753) | copy-start | bytes 589828
  94.5 10.7 %collective-permute-start.2 = (bf16[128,768]{1,0:T(8,128)(2,1)S(1)}, bf16[128,768]{1,0:T(8,128)(2,1)S(1)}, u32[]{:S(2)}, u32[]{:S(2)}) collective-permute-start(bf16[128,768]{1,0:T(8,128)(2,1)S(1)} %get-tuple-element.1753), channel_id=1, source_target_pairs={{0,1},{1,2},{2,3},{4,5},{5,6},{6,7},{8,9},{9,10},{10,11},{12,13},{... | collective-permute-start | bytes 589832 | tf_op jit(solution)/shard_map/ppermute | solution.py:21
  117.6 16.4 %copy-start.133 = (bf16[128,768]{1,0:T(8,128)(2,1)}, bf16[128,768]{1,0:T(8,128)(2,1)S(1)}, u32[]{:S(2)}) copy-start(bf16[128,768]{1,0:T(8,128)(2,1)S(1)} %get-tuple-element.1754) | copy-start | bytes 589828
  117.6 15.7 %copy-start.35 = (f32[2,128,768]{2,1,0:T(8,128)S(1)}, f32[2,128,768]{2,1,0:T(8,128)}, u32[]{:S(2)}) copy-start(f32[2,128,768]{2,1,0:T(8,128)} %copy-done.34) | copy-start | bytes 2359300
  117.6 15.7 %collective-permute-start.3 = (bf16[128,768]{1,0:T(8,128)(2,1)S(1)}, bf16[128,768]{1,0:T(8,128)(2,1)S(1)}, u32[]{:S(2)}, u32[]{:S(2)}) collective-permute-start(bf16[128,768]{1,0:T(8,128)(2,1)S(1)} %get-tuple-element.1754), channel_id=1, source_target_pairs={{0,1},{1,2},{2,3},{4,5},{5,6},{6,7},{8,9},{9,10},{10,11},{12,13},{... | collective-permute-start | bytes 589832 | tf_op jit(solution)/shard_map/ppermute | solution.py:21
  141.4 33.4 %copy-start.135 = (bf16[128,768]{1,0:T(8,128)(2,1)}, bf16[128,768]{1,0:T(8,128)(2,1)S(1)}, u32[]{:S(2)}) copy-start(bf16[128,768]{1,0:T(8,128)(2,1)S(1)} %get-tuple-element.1755) | copy-start | bytes 589828
  141.5 29.9 %collective-permute-start.4 = (bf16[128,768]{1,0:T(8,128)(2,1)S(1)}, bf16[128,768]{1,0:T(8,128)(2,1)S(1)}, u32[]{:S(2)}, u32[]{:S(2)}) collective-permute-start(bf16[128,768]{1,0:T(8,128)(2,1)S(1)} %get-tuple-element.1755), channel_id=1, source_target_pairs={{0,1},{1,2},{2,3},{4,5},{5,6},{6,7},{8,9},{9,10},{10,11},{12,13},{... | collective-permute-start | bytes 589832 | tf_op jit(solution)/shard_map/ppermute | solution.py:21
  193.2 6.9 collective-permute-start.5
  196.8 3.3 copy-start.65
  209.3 7.4 copy-start.5
  210.4 104.9 %collective-permute-start.6 = (bf16[128,768]{1,0:T(8,128)(2,1)S(1)}, bf16[128,768]{1,0:T(8,128)(2,1)S(1)}, u32[]{:S(2)}, u32[]{:S(2)}) collective-permute-start(bf16[128,768]{1,0:T(8,128)(2,1)S(1)} %convert_element_type.1345), channel_id=1, source_target_pairs={{1,0},{2,1},{3,2},{5,4},{6,5},{7,6},{9,8},{10,9},{11,10},{13,12},{... | collective-permute-start | bytes 589832 | tf_op jit(solution)/shard_map/ppermute | solution.py:21
  214.8 100.5 %copy-start.66 = (bf16[2,128,768]{2,1,0:T(8,128)(2,1)S(1)}, bf16[2,128,768]{2,1,0:T(8,128)(2,1)}, u32[]{:S(2)}) copy-start(bf16[2,128,768]{2,1,0:T(8,128)(2,1)} %param.95) | copy-start | bytes 1179652
  216.6 98.7 %copy-start.2 = (f32[128,768]{1,0:T(8,128)S(1)}, f32[128,768]{1,0:T(8,128)}, u32[]{:S(2)}) copy-start(f32[128,768]{1,0:T(8,128)} %get-tuple-element.1648) | copy-start | bytes 1179652
  216.6 98.7 %copy-start.176 = (s32[1,128]{1,0:T(1,128)S(1)}, s32[1,128]{1,0:T(1,128)}, u32[]{:S(2)}) copy-start(s32[1,128]{1,0:T(1,128)} %get-tuple-element.1654) | copy-start | bytes 1540
  218.7 96.7 %copy-start.6 = (f32[2,256,768]{2,1,0:T(8,128)}, f32[2,256,768]{2,1,0:T(8,128)S(1)}, u32[]{:S(2)}) copy-start(f32[2,256,768]{2,1,0:T(8,128)S(1)} %fusion.1187) | copy-start | bytes 4718596
  325.1 10.2 %slice-start.6 = ((s8[4718592]{0:T(1024)(128)(4,1)}), s8[4194304]{0:T(1024)(128)(4,1)S(1)}, s32[]{:S(2)}) async-start(s8[4718592]{0:T(1024)(128)(4,1)} %bitcast.945), calls=%async_computation.11 | async-start | bytes 8388608 | tf_op jit(solution)/shard_map/cond
  328.5 6.8 slice-start.7
  360.0 56.1 %copy-start.67 = (bf16[2,128,768]{2,1,0:T(8,128)(2,1)S(1)}, bf16[2,128,768]{2,1,0:T(8,128)(2,1)}, u32[]{:S(2)}) copy-start(bf16[2,128,768]{2,1,0:T(8,128)(2,1)} %param.95) | copy-start | bytes 1179652
  360.0 56.1 %copy-start.1 = (f32[128,768]{1,0:T(8,128)S(1)}, f32[128,768]{1,0:T(8,128)}, u32[]{:S(2)}) copy-start(f32[128,768]{1,0:T(8,128)} %get-tuple-element.1647) | copy-start | bytes 1179652
  360.0 56.1 %copy-start.175 = (s32[1,128]{1,0:T(1,128)S(1)}, s32[1,128]{1,0:T(1,128)}, u32[]{:S(2)}) copy-start(s32[1,128]{1,0:T(1,128)} %get-tuple-element.1662) | copy-start | bytes 1540
  361.1 55.0 %collective-permute-start.7 = (bf16[128,768]{1,0:T(8,128)(2,1)S(1)}, bf16[128,768]{1,0:T(8,128)(2,1)S(1)}, u32[]{:S(2)}, u32[]{:S(2)}) collective-permute-start(bf16[128,768]{1,0:T(8,128)(2,1)S(1)} %convert_element_type.1349), channel_id=1, source_target_pairs={{1,0},{2,1},{3,2},{5,4},{6,5},{7,6},{9,8},{10,9},{11,10},{13,12},{... | collective-permute-start | bytes 589832 | tf_op jit(solution)/shard_map/ppermute | solution.py:21
  425.8 10.2 %slice-start.8 = ((s8[4718592]{0:T(1024)(128)(4,1)}), s8[4194304]{0:T(1024)(128)(4,1)S(1)}, s32[]{:S(2)}) async-start(s8[4718592]{0:T(1024)(128)(4,1)} %bitcast.947), calls=%async_computation.13 | async-start | bytes 8388608 | tf_op jit(solution)/shard_map/cond
  429.1 6.8 slice-start.9
  460.4 7.5 copy-start.68
  460.4 7.6 copy-start
  460.4 7.6 copy-start.174
  461.5 6.4 collective-permute-start.8
  478.4 4.5 copy-start.7
  482.9 99.3 %reduce-scatter.5.cloned.1.call-start = ((), (), s32[]{:S(2)}) async-start(), calls=%async_computation.3 | async-start | bytes 983040 | tf_op jit(solution)/shard_map/reduce_scatter | solution.py:418
  489.6 307.1 %all-reduce.7.cloned.1.call-start = ((), (), s32[]{:S(2)}) async-start(), calls=%async_computation.4 | async-start | bytes 37748736 | tf_op jit(solution)/shard_map/psum | solution.py:413
  490.4 91.7 %copy-start.201 = (f32[2]{0:T(128)S(1)}, f32[2]{0:T(128)}, u32[]{:S(2)}) copy-start(f32[2]{0:T(128)} %copy-done.200) | copy-start | bytes 28
  492.0 93.3 %copy-start.136 = (bf16[128,768]{1,0:T(8,128)(2,1)S(1)}, bf16[128,768]{1,0:T(8,128)(2,1)}, u32[]{:S(2)}) copy-start(bf16[128,768]{1,0:T(8,128)(2,1)} %copy-done.135) | copy-start | bytes 589828
  492.9 93.8 %copy-start.3 = (f32[128,768]{1,0:T(8,128)S(1)}, f32[128,768]{1,0:T(8,128)}, u32[]{:S(2)}) copy-start(f32[128,768]{1,0:T(8,128)} %get-tuple-element.1402) | copy-start | bytes 1179652
  492.9 93.8 %copy-start.27 = (bf16[2,256,768]{2,1,0:T(8,128)(2,1)S(1)}, bf16[2,256,768]{2,1,0:T(8,128)(2,1)}, u32[]{:S(2)}) copy-start(bf16[2,256,768]{2,1,0:T(8,128)(2,1)} %copy-done.26) | copy-start | bytes 2359300
  492.9 93.8 %copy-start.173 = (s32[1,128]{1,0:T(1,128)S(1)}, s32[1,128]{1,0:T(1,128)}, u32[]{:S(2)}) copy-start(s32[1,128]{1,0:T(1,128)} %get-tuple-element.1657) | copy-start | bytes 1540
  584.1 27.8 %collective-permute-start.9 = (bf16[2,96,768]{2,1,0:T(8,128)(2,1)}, bf16[2,96,768]{2,1,0:T(8,128)(2,1)}, u32[]{:S(2)}, u32[]{:S(2)}) collective-permute-start(bf16[2,96,768]{2,1,0:T(8,128)(2,1)} %multiply_reduce_fusion.95), channel_id=1, source_target_pairs={{16,0},{20,4},{24,8},{28,12},{0,16},{4,20},{8,24},{12,28},{17,1},{... | collective-permute-start | bytes 884744 | tf_op jit(solution)/shard_map/ppermute | solution.py:15
  586.7 25.3 %copy-start.199 = (f32[2]{0:T(128)S(1)}, f32[2]{0:T(128)}, u32[]{:S(2)}) copy-start(f32[2]{0:T(128)} %param.92) | copy-start | bytes 28
  (10 other events, 18.3 us)
Sparse Core Ops, SparseCore 0:
  483.0 73.0 reduce-scatter.2
  558.5 23.5 reduce-scatter.4
Sparse Core Ops, SparseCore 1:
  494.8 301.8 all-reduce.6
where the time goes:
time: 830 us; the launch traced here: 817 us
  waiting for transfers between devices  453 us (55%)
  other arithmetic  79.6 us (10%)
  loops' own time  58.8 us (7%)
  starting transfers between devices  54.6 us (7%)
  matrix products  53.5 us (6%)
  local copies, waits for them, and re-layouts  50.9 us (6%)
  blocking collectives  49.8 us (6%)
  between operations  16.8 us (2%)
    psum x1, waiting for transfers between devices, on_device(): summed_mats, summed_vector = lax.psum((grad_mats, grad_vector), 'dp')  182 us
    ppermute x8, waiting for transfers between devices, shifted_2(): lax.ppermute(value, axis, [(source, source + steps) for source in range(i...  170 us
    reduce_scatter x1, waiting for transfers between devices, on_device(): lax.psum_scatter(grad_inputs.astype(jnp.bfloat16), 'section', scatter_dim...  63.2 us
    ppermute x8, starting transfers between devices, shifted_2(): lax.ppermute(value, axis, [(source, source + steps) for source in range(i...  51.9 us
    another operation x5, loops' own time, on_device(): lax.switch(jnp.where(valid, kind, 0), [spare_backward, self_backward, mer...  41.6 us
    add x2, other arithmetic, backward_mlp(): grad_mats + jnp.stack([grad_first, grad_second])  29.9 us
    reduce_scatter x1, waiting for transfers between devices, on_device(): lax.psum_scatter(grad_sources.astype(jnp.bfloat16), 'section', scatter_di...  26 us
    dot_general x4, matrix products, times_transposed(): lax.dot_general(multiplier, multiplicand, (((1,), (1,)), ((), ())), prefe...  22.4 us
  transfers between devices with their start and end apart: 13, of which 12 were waited for; matrix products, arithmetic and copies ran while one was open for 6% of the time, Pallas kernels for 0%

commit v1 on v0

v1 whole, which is shorter than its diff:
```python
from functools import partial

import jax
import jax.numpy as jnp
from jax import lax
from jax.experimental import pallas as pl
from jax.experimental.pallas import tpu as pltpu
from jax.sharding import PartitionSpec as P

HEAD = 64
PAIR = 2 * HEAD
MESH = pl.DeviceIdType.MESH
bf16 = jnp.bfloat16
f32 = jnp.float32


def dot(a, b):
    return lax.dot_general(a, b, (((1,), (0,)), ((), ())), preferred_element_type=f32)


def dot_t(a, b):
    return lax.dot_general(a, b, (((1,), (1,)), ((), ())), preferred_element_type=f32)


def t_dot(a, b):
    return lax.dot_general(a, b, (((0,), (0,)), ((), ())), preferred_element_type=f32)


def row_mean(x):
    return jnp.sum(x, axis=-1, keepdims=True) * (1.0 / x.shape[-1])


def normalize(h):
    center = h - row_mean(h)
    scale = lax.rsqrt(row_mean(center * center) + 1e-06)
    return center * scale, scale


def normalize_back(grad, unit, scale, gain):
    inner = grad * gain
    return scale * (inner - row_mean(inner) - unit * row_mean(inner * unit))


def gelu_parts(a):
    cdf = 0.5 * (1.0 + lax.erf(a * (0.5**0.5)))
    pdf = jnp.exp(a * a * (-0.5)) * 0.3989422804014327
    return a * cdf, cdf + a * pdf


def halves(x):
    low = lax.broadcasted_iota(jnp.int32, x.shape, 1) < HEAD
    zero = jnp.zeros_like(x)
    return jnp.concatenate([jnp.where(low, x, zero), jnp.where(low, zero, x)], axis=0)


def softmax(scores, allowed):
    scores = jnp.where(allowed, scores, -1000000000.0)
    weights = jnp.exp(scores - jnp.max(scores, axis=-1, keepdims=True))
    return weights * (1.0 / jnp.sum(weights, axis=-1, keepdims=True))


def attend_pair(q, k, v, allowed):
    n = k.shape[0]
    scores = dot_t(q, halves(k))
    weights = jnp.concatenate(
        [softmax(scores[:, :n], allowed), softmax(scores[:, n:], allowed)], axis=1
    )
    return dot(weights.astype(bf16), halves(v)), weights


def attend_pair_back(q, k, v, weights, grad):
    n = k.shape[0]
    grad_weights = dot_t(grad, halves(v))
    product = weights * grad_weights
    parts = []
    for part in (slice(0, n), slice(n, 2 * n)):
        total = jnp.sum(product[:, part], axis=-1, keepdims=True)
        parts.append((product[:, part] - weights[:, part] * total).astype(bf16))
    grad_q = dot(jnp.concatenate(parts, axis=1), halves(k)) * (HEAD**-0.5)
    grad_k = t_dot(jnp.concatenate(parts, axis=0), halves(q))
    rounded = weights.astype(bf16)
    grad_v = t_dot(jnp.concatenate([rounded[:, :n], rounded[:, n:]], axis=0), halves(grad))
    return grad_q, grad_k, grad_v


def column_sum(x):
    return jnp.sum(x.astype(f32), axis=0, keepdims=True)


def kernel(names, *refs):
    R = dict(zip(names, refs))
    inputs, other_view, mats, vec = (R[k] for k in ("inputs", "other_view", "mats", "vec"))
    mixing, partner, cot = R["mixing"], R["partner"], R["cot"]
    seg_q, seg_k, seg_v = R["seg_q"], R["seg_k"], R["seg_v"]
    records, in_grad, view_grad = R["records"], R["in_grad"], R["view_grad"]
    G, gv = R["G"], R["gv"]
    w, hin, gin, gout = R["w"], R["hin"], R["gin"], R["gout"]
    B, TS, D = inputs.shape
    VS = other_view.shape[1]
    T = records.shape[1]
    S = lax.axis_size("section")
    n_dp = lax.axis_size("dp")
    z = lax.axis_index("section")
    d = lax.axis_index("dp")
    far = {"dp": lax.rem(d + n_dp // 2, n_dp)}
    pairs = D // PAIR

    def remote(src, dst, send, recv, device):
        return pltpu.make_async_remote_copy(
            src_ref=src,
            dst_ref=dst,
            send_sem=send,
            recv_sem=recv,
            device_id=device,
            device_id_type=MESH,
        )

    def table(t):
        return pltpu.make_async_copy(mats.at[0, t], w.at[t], R["w_sem"].at[t])

    table(0).start()
    table(1).start()

    barrier = pltpu.get_barrier_semaphore()
    pl.semaphore_signal(barrier, inc=1, device_id=far, device_id_type=MESH)
    for o in range(1, S):
        pl.semaphore_signal(
            barrier, inc=1, device_id={"section": lax.rem(z + o, S)}, device_id_type=MESH
        )
    pl.semaphore_wait(barrier, S)

    ex = R["ex_sem"]
    far_i = remote(inputs, R["far_i"], ex.at[0], ex.at[1], far)
    far_v = remote(other_view, R["far_v"], ex.at[2], ex.at[3], far)
    far_i.start()
    far_v.start()
    gv[...] = jnp.zeros_like(gv)
    pick = [[(partner[r] == j).astype(f32) for j in range(B)] for r in range(B)]
    mix = [mixing[r] for r in range(B)]

    def blend(own, other, r):
        chosen = sum(pick[r][j] * other[j].astype(f32) for j in range(B))
        return (mix[r] * own[r].astype(f32) + (1.0 - mix[r]) * chosen).astype(bf16)

    def gather_i(r, source):
        return remote(
            R["stage_i"].at[r],
            hin.at[r, pl.ds(source * TS, TS)],
            R["gi_send"].at[r],
            R["gi_recv"].at[r, source],
            {"section": 0},
        )

    def gather_v(r, source):
        return remote(
            R["stage_v"].at[r],
            R["view"].at[r, pl.ds(source * VS, VS)],
            R["gv_send"].at[r],
            R["gv_recv"].at[r, source],
            {"section": 2},
        )

    far_i.wait_recv()
    for r in range(B):
        mixed = blend(inputs, R["far_i"], r)

        @pl.when(z == 0)
        def _():
            hin[r, :TS] = mixed

        @pl.when(z != 0)
        def _():
            R["stage_i"][r] = mixed
            gather_i(r, z).start()

    far_v.wait_recv()
    for r in range(B):
        mixed_view = blend(other_view, R["far_v"], r)

        @pl.when(z == 2)
        def _():
            R["view"][r, 2 * VS : 3 * VS] = mixed_view

        @pl.when(z != 2)
        def _():
            R["stage_v"][r] = mixed_view
            gather_v(r, z).start()

    far_i.wait_send()
    far_v.wait_send()

    def forward_hop(r):
        return remote(
            records.at[r], hin.at[r], R["f_send"].at[r], R["f_recv"].at[r], {"section": z + 1}
        )

    def backward_hop(r):
        return remote(
            gout.at[r], gin.at[r], R["b_send"].at[r], R["b_recv"].at[r], {"section": z - 1}
        )

    def entered(r):
        remote(
            hin.at[r], hin.at[r], R["f_send"].at[r], R["f_recv"].at[r], {"section": z - 1}
        ).wait_recv()

    def returned(r):
        remote(
            gin.at[r], gin.at[r], R["b_send"].at[r], R["b_recv"].at[r], {"section": z + 1}
        ).wait_recv()

    def each_row(step):
        lax.fori_loop(0, B, lambda r, c: (step(r), c)[1], 0)

    def cols(b, width=D):
        return slice(b * width, (b + 1) * width)

    def flat(x):
        return x[...].reshape(B * T, x.shape[2])

    def norm_in(h, r, unit, scale, normed, gain, shift):
        unit_value, scale_value = normalize(h)
        unit[r] = unit_value
        scale[r] = scale_value
        value = (unit_value * vec[gain : gain + 1] + vec[shift : shift + 1]).astype(bf16)
        normed[r] = value
        return value

    def norm_out(grad, r, unit, scale, gain):
        return normalize_back(grad, unit[r], scale[r], vec[gain : gain + 1])

    def norm_sums(grad, r, unit, gain, shift):
        gv[gain : gain + 1] += column_sum(grad * unit[r])
        gv[shift : shift + 1] += column_sum(grad)

    def self_attend(r, qkv, weights, attended):
        allowed = seg_q[r] == seg_k[r]
        for p in range(pairs):
            c = cols(p, PAIR)
            k = slice(D + c.start, D + c.stop)
            v = slice(2 * D + c.start, 2 * D + c.stop)
            out, kept = attend_pair(qkv[r, :, c], qkv[r, :, k], qkv[r, :, v], allowed)
            attended[r, :, c] = out.astype(bf16)
            weights[r, p] = kept

    def self_attend_back(r, qkv, weights, grad, dqkv):
        for p in range(pairs):
            c = cols(p, PAIR)
            k = slice(D + c.start, D + c.stop)
            v = slice(2 * D + c.start, 2 * D + c.stop)
            dq, dk, dv = attend_pair_back(
                qkv[r, :, c], qkv[r, :, k], qkv[r, :, v], weights[r, p], grad[r, :, c]
            )
            dqkv[r, :, c] = dq.astype(bf16)
            dqkv[r, :, k] = dk.astype(bf16)
            dqkv[r, :, v] = dv.astype(bf16)

    n1, u1, s1, p1, a1 = R["n1"], R["u1"], R["s1"], R["p1"], R["a1"]
    qkv1, dqkv1, do1 = R["qkv1"], R["dqkv1"], R["do1"]
    n2, u2, s2, p2, a2 = R["n2"], R["u2"], R["s2"], R["p2"], R["a2"]
    q2, dq2, kv2, dkv2, do2 = R["q2"], R["dq2"], R["kv2"], R["dkv2"], R["do2"]
    view, dm = R["view"], R["dm"]
    g, gp, da = R["g"], R["gp"], R["da"]
    SCALE = HEAD**-0.5

    @pl.when(z == 0)
    def _():
        table(0).wait()
        table(1).wait()

        def forward(r):
            for k in range(1, S):
                gather_i(r, k).wait_recv()
            h = hin[r].astype(f32)
            n = norm_in(h, r, u1, s1, n1, 0, 1)
            q = (dot(n, w[0, :, cols(0)]) + vec[5:6]).astype(bf16)
            qkv1[r, :, cols(0)] = q * SCALE
            qkv1[r, :, cols(1)] = dot(n, w[0, :, cols(1)]).astype(bf16)
            qkv1[r, :, cols(2)] = (dot(n, w[0, :, cols(2)]) + vec[2:3]).astype(bf16)
            self_attend(r, qkv1, p1, a1)
            out = h + dot(a1[r], w[0, :, cols(3)]) + vec[4:5]
            records[r] = out.astype(bf16)
            forward_hop(r).start()

        each_row(forward)

        def backward(r):
            returned(r)
            e = gin[r]
            do1[r] = dot_t(e, w[0, :, cols(3)]).astype(bf16)
            self_attend_back(r, qkv1, p1, do1, dqkv1)
            dn = dot_t(dqkv1[r], w[0, :, : 3 * D])
            gout[r] = (e.astype(f32) + norm_out(dn, r, u1, s1, 0)).astype(bf16)
            norm_sums(dn, r, u1, 0, 1)
            gv[2:3] += column_sum(dqkv1[r, :, cols(2)])
            gv[4:5] += column_sum(e)
            gv[5:6] += column_sum(dqkv1[r, :, cols(0)])

        each_row(backward)
        G[3] = t_dot(flat(a1), flat(gin)).astype(bf16)
        for b in range(3):
            G[b] = t_dot(flat(n1), dqkv1[:, :, cols(b)].reshape(B * T, D)).astype(bf16)
        for b in range(4, 8):
            G[b] = jnp.zeros_like(G[b])

    def feed_hidden(n, c):
        a = dot(n, w[0, :, cols(c)]) + vec[2 + c : 3 + c]
        return gelu_parts(a)

    def feed_grads(e_rows):
        def one(c, _):
            cc = pl.ds(pl.multiple_of(c * D, D), D)
            G[4 + c] = t_dot(flat(e_rows), g[:, :, cc].reshape(B * T, D)).astype(bf16)
            G[c] = t_dot(flat(n1), da[:, :, cc].reshape(B * T, D)).astype(bf16)
            return 0

        lax.fori_loop(0, 4, one, 0)

    def feed_sums(r, e):
        for c in range(4):
            gv[2 + c : 3 + c] += column_sum(da[r, :, cols(c)])
        gv[6:7] += column_sum(e)

    @pl.when(z == 1)
    def _():
        table(0).wait()
        table(1).wait()

        def forward(r):
            entered(r)
            h = hin[r].astype(f32)
            n = norm_in(h, r, u1, s1, n1, 0, 1)
            out = h + vec[6:7]
            for c in range(4):
                active, slope = feed_hidden(n, c)
                active = active.astype(bf16)
                g[r, :, cols(c)] = active
                gp[r, :, cols(c)] = slope
                out += dot_t(active, w[1, :, cols(c)])
            records[r] = out.astype(bf16)
            forward_hop(r).start()

        each_row(forward)

        def backward(r):
            returned(r)
            e = gin[r]
            dn = jnp.zeros((T, D), f32)
            for c in range(4):
                dg = dot(e, w[1, :, cols(c)])
                dc = (dg * gp[r, :, cols(c)]).astype(bf16)
                da[r, :, cols(c)] = dc
                dn += dot_t(dc, w[0, :, cols(c)])
            gout[r] = (e.astype(f32) + norm_out(dn, r, u1, s1, 0)).astype(bf16)
            backward_hop(r).start()
            norm_sums(dn, r, u1, 0, 1)
            feed_sums(r, e)

        each_row(backward)
        feed_grads(gin)

    @pl.when(z == 3)
    def _():
        table(0).wait()
        table(1).wait()

        def ahead(r):
            e = cot[r]
            for c in range(4):
                gp[r, :, cols(c)] = dot(e, w[1, :, cols(c)])

        each_row(ahead)

        def turn(r):
            entered(r)
            e = cot[r]
            n = norm_in(hin[r].astype(f32), r, u1, s1, n1, 0, 1)
            dn = jnp.zeros((T, D), f32)
            for c in range(4):
                active, slope = feed_hidden(n, c)
                g[r, :, cols(c)] = active.astype(bf16)
                dc = (gp[r, :, cols(c)] * slope).astype(bf16)
                da[r, :, cols(c)] = dc
                dn += dot_t(dc, w[0, :, cols(c)])
            gout[r] = (e.astype(f32) + norm_out(dn, r, u1, s1, 0)).astype(bf16)
            backward_hop(r).start()
            norm_sums(dn, r, u1, 0, 1)
            feed_sums(r, e)

        each_row(turn)

        def output(r):
            records[r] = (hin[r].astype(f32) + dot_t(g[r], w[1]) + vec[6:7]).astype(bf16)

        each_row(output)
        feed_grads(cot)

    @pl.when(z == 2)
    def _():
        table(0).wait()
        table(1).wait()

        def ahead(r):
            for k in (0, 1, 3):
                gather_v(r, k).wait_recv()
            for b in range(2):
                kv2[r, :, cols(b)] = dot(view[r], w[0, :, cols(1 + b)]).astype(bf16)

        each_row(ahead)

        def forward(r):
            entered(r)
            h = hin[r].astype(f32)
            n = norm_in(h, r, u2, s2, n2, 0, 1)
            q2[r] = dot(n, w[0, :, cols(0)]).astype(bf16) * SCALE
            allowed = seg_q[r] == seg_v[r]
            for p in range(pairs):
                c = cols(p, PAIR)
                v = slice(D + c.start, D + c.stop)
                out, kept = attend_pair(q2[r, :, c], kv2[r, :, c], kv2[r, :, v], allowed)
                a2[r, :, c] = out.astype(bf16)
                p2[r, p] = kept
            m = h + dot(a2[r], w[0, :, cols(3)]) + vec[4:5]
            n = norm_in(m, r, u1, s1, n1, 2, 3)
            q = (dot(n, w[1, :, cols(0)]) + vec[5:6]).astype(bf16)
            qkv1[r, :, cols(0)] = q * SCALE
            qkv1[r, :, cols(1)] = dot(n, w[1, :, cols(1)]).astype(bf16)
            qkv1[r, :, cols(2)] = dot(n, w[1, :, cols(2)]).astype(bf16)
            self_attend(r, qkv1, p1, a1)
            out = m + dot(a1[r], w[1, :, cols(3)]) + vec[6:7]
            records[r] = out.astype(bf16)
            forward_hop(r).start()

        each_row(forward)

        def backward(r):
            returned(r)
            e = gin[r]
            do1[r] = dot_t(e, w[1, :, cols(3)]).astype(bf16)
            self_attend_back(r, qkv1, p1, do1, dqkv1)
            dn = dot_t(dqkv1[r], w[1, :, : 3 * D])
            dmid = e.astype(f32) + norm_out(dn, r, u1, s1, 2)
            dm[r] = dmid.astype(bf16)
            norm_sums(dn, r, u1, 2, 3)
            gv[4:5] += column_sum(dmid)
            gv[5:6] += column_sum(dqkv1[r, :, cols(0)])
            gv[6:7] += column_sum(e)
            do2[r] = dot_t(dm[r], w[0, :, cols(3)]).astype(bf16)
            for p in range(pairs):
                c = cols(p, PAIR)
                v = slice(D + c.start, D + c.stop)
                dq, dk, dv = attend_pair_back(
                    q2[r, :, c], kv2[r, :, c], kv2[r, :, v], p2[r, p], do2[r, :, c]
                )
                dq2[r, :, c] = dq.astype(bf16)
                dkv2[r, :, c] = dk.astype(bf16)
                dkv2[r, :, v] = dv.astype(bf16)
            dn = dot_t(dq2[r], w[0, :, cols(0)])
            gout[r] = (dmid + norm_out(dn, r, u2, s2, 0)).astype(bf16)
            backward_hop(r).start()
            norm_sums(dn, r, u2, 0, 1)

        each_row(backward)

        def source_grad(r):
            R["dw"][r] = dot_t(dkv2[r], w[0, :, D : 3 * D]).astype(bf16)

        each_row(source_grad)
        G[7] = t_dot(flat(a1), flat(gin)).astype(bf16)
        for b in range(3):
            G[4 + b] = t_dot(flat(n1), dqkv1[:, :, cols(b)].reshape(B * T, D)).astype(bf16)
        G[3] = t_dot(flat(a2), flat(dm)).astype(bf16)
        G[0] = t_dot(flat(n2), flat(dq2)).astype(bf16)
        for b in range(2):
            wide = view.shape[1]
            G[1 + b] = t_dot(
                view[...].reshape(B * wide, D), dkv2[:, :, cols(b)].reshape(B * wide, D)
            ).astype(bf16)

    part_i, part_v = R["part_i"], R["part_v"]

    def scatter_i(k):
        return remote(
            gout.at[:, pl.ds(k * TS, TS)],
            part_i,
            R["si_send"].at[k],
            R["s_recv"].at[0],
            {"section": k},
        )

    def scatter_v(k):
        return remote(
            R["dw"].at[:, pl.ds(k * VS, VS)],
            part_v,
            R["sv_send"].at[k],
            R["s_recv"].at[1],
            {"section": k},
        )

    @pl.when(z == 0)
    def _():
        for k in range(1, S):
            scatter_i(k).start()
        part_i[...] = gout[:, :TS]

    @pl.when(z == 2)
    def _():
        for k in (0, 1, 3):
            scatter_v(k).start()
        part_v[...] = R["dw"][:, 2 * VS : 3 * VS]

    @pl.when(z != 0)
    def _():
        scatter_i(0).wait_recv()

    @pl.when(z != 2)
    def _():
        scatter_v(0).wait_recv()

    owed_i, owed_v = R["owed_i"], R["owed_v"]
    back = []
    for part, owed, arrive, s in (
        (part_i, owed_i, R["arr_i"], 4),
        (part_v, owed_v, R["arr_v"], 6),
    ):
        for t in range(B):
            owed[t] = sum(
                pick[r][t] * (1.0 - mix[r]) * part[r].astype(f32) for r in range(B)
            ).astype(bf16)
        copy = remote(owed, arrive, ex.at[s], ex.at[s + 1], far)
        copy.start()
        back.append(copy)
    for copy, part, arrive, out in (
        (back[0], part_i, R["arr_i"], in_grad),
        (back[1], part_v, R["arr_v"], view_grad),
    ):
        copy.wait_recv()
        for r in range(B):
            out[r] = (mix[r] * part[r].astype(f32) + arrive[r].astype(f32)).astype(bf16)
        copy.wait_send()

    @pl.when(z == 0)
    def _():
        for k in range(1, S):
            scatter_i(k).wait_send()

    @pl.when(z == 2)
    def _():
        for k in (0, 1, 3):
            scatter_v(k).wait_send()

    for r in range(B):

        @pl.when(z != 0)
        def _():
            gather_i(r, z).wait_send()
            backward_hop(r).wait_send()

        @pl.when(z != 2)
        def _():
            gather_v(r, z).wait_send()

        @pl.when(z != S - 1)
        def _():
            forward_hop(r).wait_send()


def on_device(inputs, other_view, mats, vectors, mixing, partner, segments, cotangent):
    B, TS, D = inputs.shape
    VS = other_view.shape[1]
    T = segments.shape[1]
    S = lax.axis_size("section")
    V = VS * S
    H = mats.shape[3]
    pairs = D // PAIR
    vmem = pl.BlockSpec(memory_space=pltpu.VMEM)
    smem = pl.BlockSpec(memory_space=pltpu.SMEM)
    hbm = pl.BlockSpec(memory_space=pl.ANY)
    args = {
        "inputs": (inputs, vmem),
        "other_view": (other_view, vmem),
        "mats": (mats, hbm),
        "vec": (vectors[0], vmem),
        "mixing": (mixing, smem),
        "partner": (partner, smem),
        "seg_q": (segments[:, :, None], vmem),
        "seg_k": (segments[:, None, :], vmem),
        "seg_v": (jnp.repeat(segments, V // T, axis=1)[:, None, :], vmem),
        "cot": (cotangent, vmem),
    }
    outs = {
        "records": (B, T, D, bf16),
        "in_grad": (B, TS, D, bf16),
        "view_grad": (B, VS, D, bf16),
        "G": (8, D, D, bf16),
        "gv": (8, D, f32),
    }
    dma = pltpu.SemaphoreType.DMA

    def buf(*shape, dtype=bf16):
        return pltpu.VMEM(shape, dtype)

    scratch = {
        "w": buf(2, D, H),
        "hin": buf(B, T, D),
        "gin": buf(B, T, D),
        "gout": buf(B, T, D),
        "far_i": buf(B, TS, D),
        "far_v": buf(B, VS, D),
        "stage_i": buf(B, TS, D),
        "stage_v": buf(B, VS, D),
        "part_i": buf(B, TS, D),
        "part_v": buf(B, VS, D),
        "owed_i": buf(B, TS, D),
        "owed_v": buf(B, VS, D),
        "arr_i": buf(B, TS, D),
        "arr_v": buf(B, VS, D),
        "view": buf(B, V, D),
        "dw": buf(B, V, D),
        "n1": buf(B, T, D),
        "u1": buf(B, T, D, dtype=f32),
        "s1": buf(B, T, 1, dtype=f32),
        "p1": buf(B, pairs, T, 2 * T, dtype=f32),
        "a1": buf(B, T, D),
        "qkv1": buf(B, T, 3 * D),
        "dqkv1": buf(B, T, 3 * D),
        "do1": buf(B, T, D),
        "n2": buf(B, T, D),
        "u2": buf(B, T, D, dtype=f32),
        "s2": buf(B, T, 1, dtype=f32),
        "p2": buf(B, pairs, T, 2 * V, dtype=f32),
        "a2": buf(B, T, D),
        "q2": buf(B, T, D),
        "dq2": buf(B, T, D),
        "kv2": buf(B, V, 2 * D),
        "dkv2": buf(B, V, 2 * D),
        "do2": buf(B, T, D),
        "dm": buf(B, T, D),
        "g": buf(B, T, H),
        "gp": buf(B, T, H, dtype=f32),
        "da": buf(B, T, H),
        "w_sem": dma((2,)),
        "ex_sem": dma((8,)),
        "gi_send": dma((B,)),
        "gi_recv": dma((B, S)),
        "gv_send": dma((B,)),
        "gv_recv": dma((B, S)),
        "f_send": dma((B,)),
        "f_recv": dma((B,)),
        "b_send": dma((B,)),
        "b_recv": dma((B,)),
        "si_send": dma((S,)),
        "sv_send": dma((S,)),
        "s_recv": dma((2,)),
    }
    names = list(args) + list(outs) + list(scratch)
    records, in_grad, view_grad, G, gv = pl.pallas_call(
        partial(kernel, names),
        out_shape=[jax.ShapeDtypeStruct(s[:-1], s[-1]) for s in outs.values()],
        in_specs=[spec for _, spec in args.values()],
        out_specs=[vmem] * len(outs),
        scratch_shapes=list(scratch.values()),
        compiler_params=pltpu.CompilerParams(
            collective_id=0, has_side_effects=True, vmem_limit_bytes=60 << 20
        ),
        name="relay",
    )(*[value for value, _ in args.values()])
    total = lax.psum(G, "dp").astype(f32)
    total = total.reshape(2, 4, D, D).transpose(0, 2, 1, 3).reshape(mats.shape)
    summed = lax.psum(gv[: vectors.shape[1]], "dp")
    return records[None], in_grad, view_grad, total, summed[None]


def solution(mesh):
    in_specs = (
        P("dp", "section", None),
        P("dp", "section", None),
        P("section", None, None, None),
        P("section", None, None),
        P("dp"),
        P("dp"),
        P("dp", None),
        P("dp", None, None),
    )
    out_specs = (
        P("section", "dp", None, None),
        P("dp", "section", None),
        P("dp", "section", None),
        P("section", None, None, None),
        P("section", None, None),
    )
    return jax.shard_map(
        on_device, mesh=mesh, in_specs=in_specs, out_specs=out_specs, check_vma=False
    )
```

time: 830 us -> 303 us (0.37); the launches traced: 817 us -> 301 us
  waiting for transfers between devices: 453 us -> 120 us
  Pallas kernels: 0 us -> 87.4 us
  other arithmetic: 79.6 us -> 12.7 us
  loops' own time: 58.8 us -> 0 us
  starting transfers between devices: 54.6 us -> 0.04 us
  matrix products: 53.5 us -> 0 us
  blocking collectives: 49.8 us -> 29.9 us
  local copies, waits for them, and re-layouts: 50.9 us -> 36.9 us
    ppermute x10 -> x0, waiting for transfers between devices: 181 us -> none  [the longest x8 170 us: shifted_2(): lax.ppermute(value, axis, [(source, source + steps) for source in range(i...]
    reduce_scatter x2 -> x0, waiting for transfers between devices: 89.2 us -> none  [the longest x1 63.2 us: on_device(): lax.psum_scatter(grad_inputs.astype(jnp.bfloat16), 'section', scatter_dim...]
    pallas_call x0 -> x1, Pallas kernels: none -> 87.4 us  [on_device(): pl.pallas_call(partial(kernel, names), out_shape=[jax.ShapeDtypeStruct(s[...]
    psum x1, waiting for transfers between devices: 182 us -> 119 us  [on_device(): total = lax.psum(G, 'dp').astype(f32)]
    another operation x10 -> x0, loops' own time: 58.8 us -> none  [the longest x5 41.6 us: on_device(): lax.switch(jnp.where(valid, kind, 0), [spare_backward, self_backward, mer...]
    ppermute x10 -> x0, starting transfers between devices: 54.4 us -> none  [the longest x8 51.9 us: shifted_2(): lax.ppermute(value, axis, [(source, source + steps) for source in range(i...]
    dot_general x12 -> x0, matrix products: 53.5 us -> none  [the longest x4 22.4 us: times_transposed(): lax.dot_general(multiplier, multiplicand, (((1,), (1,)), ((), ())), prefe...]
    add x5 -> x0, other arithmetic: 30.5 us -> none  [the longest x2 29.9 us: backward_mlp(): grad_mats + jnp.stack([grad_first, grad_second])]
  transfers between devices with their start and end apart: 13 -> 1, of which waited for: 12 -> 1; matrix products, arithmetic and copies ran while one was open for 6% -> 0% of each run, Pallas kernels for 0% -> 0%
where the time goes in v1:
time: 303 us; the launch traced here: 301 us
  waiting for transfers between devices  120 us (40%)
  Pallas kernels  87.4 us (29%)
  local copies, waits for them, and re-layouts  36.9 us (12%)
  blocking collectives  29.9 us (10%)
  between operations  14.1 us (5%)
  other arithmetic  12.7 us (4%)
    psum x1, waiting for transfers between devices, on_device(): total = lax.psum(G, 'dp').astype(f32)  119 us
    pallas_call x1, Pallas kernels, on_device(): pl.pallas_call(partial(kernel, names), out_shape=[jax.ShapeDtypeStruct(s[...  87.4 us
    psum x1, blocking collectives, on_device(): summed = lax.psum(gv[:vectors.shape[1]], 'dp')  29.9 us
    reshape x1, local copies, waits for them, and re-layouts, on_device(): total = total.reshape(2, 4, D, D).transpose(0, 2, 1, 3).reshape(mats.shape)  16.9 us
    reshape x1, other arithmetic, on_device(): total = total.reshape(2, 4, D, D).transpose(0, 2, 1, 3).reshape(mats.shape)  12.7 us
    transpose x1, local copies, waits for them, and re-layouts, on_device(): total = total.reshape(2, 4, D, D).transpose(0, 2, 1, 3).reshape(mats.shape)  12.3 us
  transfers between devices with their start and end apart: 1, of which 1 were waited for; matrix products, arithmetic and copies ran while one was open for 0% of the time, Pallas kernels for 0%

profile of v1, /device:TPU:9, one launch (start us, length us, event | category | flops | bytes accessed | tf_op | source)
XLA Modules:
  0.0 300.5 jit_solution(11171174124608705363)
XLA Ops:
  7.2 0.0 all-reduce.2.cloned.1.call-start
  7.2 1.3 copy.21
  8.6 1.5 copy.15.refs_6_
  10.0 0.8 broadcast_in_dim.17
  10.8 0.7 broadcast_in_dim_reshape.4.refs_8_
  11.5 87.4 %relay.1 = (bf16[2,128,768]{2,1,0:T(8,128)(2,1)}, bf16[2,32,768]{2,1,0:T(8,128)(2,1)}, bf16[2,64,768]{2,1,0:T(8,128)(2,1)}, bf16[8,768,768]{2,1,0:T(8,128)(2,1)}, f32[8,768]{1,0:T(8,128)}) custom-call(bf16[2,32,768]{2,1,0:T(8,128)(2,1)} %refs_0_.1, bf16[2,64,768]{2,1,0:T(8,128)(2,1)} %refs_1_.1, bf16[1,2,768,3072]{3,2,1,0:T(8,128)(2,1)} %refs_2_.1, ...), custom_call_target="tpu_custom_call" | custom-call | tf_op jit(solution)/shard_map/relay/pallas_call | solution.py:657
  98.9 12.3 %copy.17 = bf16[2,768,4,768]{3,2,1,0:T(4,128)(2,1)} copy(bf16[2,768,4,768]{3,1,2,0:T(8,128)(2,1)} %bitcast.11) | data formatting | bytes 18874368 | tf_op jit(solution)/shard_map/transpose | solution.py:669
  111.2 16.9 %reshape.21 = bf16[1,2,768,3072]{3,2,1,0:T(8,128)(2,1)} reshape(bf16[2,768,4,768]{3,2,1,0:T(4,128)(2,1)} %copy.17) | data formatting | bytes 18874368 | tf_op jit(solution)/shard_map/reshape | solution.py:669
  128.1 0.0 copy-start.3
  128.1 0.0 all-reduce.2.cloned.1.call-update
  128.1 0.7 copy-done.3
  128.8 29.9 %psum.15 = f32[1,7,768]{2,1,0:T(8,128)S(1)} all-reduce(f32[1,7,768]{2,1,0:T(8,128)S(1)} %slice_bitcast_fusion), channel_id=1, replica_groups=mesh['dp'=8,'section'=4] {'dp'}, use_global_device_ids=true, to_apply=%region_1.0 | all-reduce | flops 5376 | bytes 43008 | tf_op jit(solution)/shard_map/psum | solution.py:670
  158.8 0.6 copy.18
  159.4 0.0 copy-start
  159.4 0.0 copy-start.2
  159.4 0.0 copy-start.1
  159.4 119.5 %all-reduce.2.cloned.1.call-done = bf16[1,2,768,3072]{3,2,1,0:T(8,128)(2,1)} async-done(((bf16[1,2,768,3072]{3,2,1,0:T(8,128)(2,1)}), bf16[1,2,768,3072]{3,2,1,0:T(8,128)(2,1)}) %all-reduce.2.cloned.1.call-update) | async-done | bytes 9437200 | tf_op jit(solution)/shard_map/psum | solution.py:668
  278.9 12.7 %reshape.22 = f32[1,2,768,3072]{3,2,1,0:T(8,128)} convert(bf16[1,2,768,3072]{3,2,1,0:T(8,128)(2,1)} %all-reduce.2.cloned.1.call-done) | non-fusion elementwise | flops 4718592 | bytes 28311552 | tf_op jit(solution)/shard_map/reshape | solution.py:669
  291.6 0.0 copy-done
  291.6 0.7 copy.26
  292.4 0.0 copy-done.2
  292.4 0.6 copy.27
  293.0 0.0 copy-done.1
  293.0 0.7 copy.28
  (1 shorter events, 0.0 us)
Async XLA Ops:
  7.2 271.8 %all-reduce.2.cloned.1.call-start = ((), (), s32[]{:S(2)}) async-start(), calls=%async_computation | async-start | bytes 18874368 | tf_op jit(solution)/shard_map/psum | solution.py:668
  128.1 0.7 copy-start.3
  159.4 132.2 %copy-start = (bf16[2,128,768]{2,1,0:T(8,128)(2,1)S(1)}, bf16[2,128,768]{2,1,0:T(8,128)(2,1)}, u32[]{:S(2)}) copy-start(bf16[2,128,768]{2,1,0:T(8,128)(2,1)} %get-tuple-element.10) | copy-start | bytes 1179652
  159.4 133.0 %copy-start.2 = (bf16[2,32,768]{2,1,0:T(8,128)(2,1)S(1)}, bf16[2,32,768]{2,1,0:T(8,128)(2,1)}, u32[]{:S(2)}) copy-start(bf16[2,32,768]{2,1,0:T(8,128)(2,1)} %get-tuple-element.31) | copy-start | bytes 294916
  159.4 133.6 %copy-start.1 = (bf16[2,64,768]{2,1,0:T(8,128)(2,1)S(1)}, bf16[2,64,768]{2,1,0:T(8,128)(2,1)}, u32[]{:S(2)}) copy-start(bf16[2,64,768]{2,1,0:T(8,128)(2,1)} %get-tuple-element.32) | copy-start | bytes 589828
Sparse Core Ops, SparseCore 0:
  128.3 150.6 all-reduce.1

commit v2 on v1

--- a/solution.py
+++ b/solution.py
@@ -87,14 +87,14 @@
     return jnp.sum(x.astype(f32), axis=0, keepdims=True)
 
 
-def kernel(names, *refs):
+def kernel(names, fused, *refs):
     R = dict(zip(names, refs))
     inputs, other_view, mats, vec = (R[k] for k in ("inputs", "other_view", "mats", "vec"))
     mixing, partner, cot = R["mixing"], R["partner"], R["cot"]
-    seg_q, seg_k, seg_v = R["seg_q"], R["seg_k"], R["seg_v"]
+    segments, seg_q, seg_v = R["segments"], R["seg_q"], R["seg_v"]
     records, in_grad, view_grad = R["records"], R["in_grad"], R["view_grad"]
-    G, gv = R["G"], R["gv"]
-    w, hin, gin, gout = R["w"], R["hin"], R["gin"], R["gout"]
+    G, gv, w = R["G"], R["gv"], R["w"]
+    hin, gin, gout = R["hin"], R["gin"], R["gout"]
     B, TS, D = inputs.shape
     VS = other_view.shape[1]
     T = records.shape[1]
@@ -104,6 +104,9 @@
     d = lax.axis_index("dp")
     far = {"dp": lax.rem(d + n_dp // 2, n_dp)}
     pairs = D // PAIR
+    core, x_bit, y_bit = lax.rem(d, 2), lax.rem(d // 2, 2), d // 4
+    beside = {"dp": d + 1 - 2 * core}
+    x_next = {"dp": d + 2 - 4 * x_bit}
 
     def remote(src, dst, send, recv, device):
         return pltpu.make_async_remote_copy(
@@ -122,12 +125,12 @@
     table(1).start()
 
     barrier = pltpu.get_barrier_semaphore()
-    pl.semaphore_signal(barrier, inc=1, device_id=far, device_id_type=MESH)
-    for o in range(1, S):
-        pl.semaphore_signal(
-            barrier, inc=1, device_id={"section": lax.rem(z + o, S)}, device_id_type=MESH
-        )
-    pl.semaphore_wait(barrier, S)
+    others = [far] + [{"section": lax.rem(z + o, S)} for o in range(1, S)]
+    if fused:
+        others += [beside, x_next]
+    for other in others:
+        pl.semaphore_signal(barrier, inc=1, device_id=other, device_id_type=MESH)
+    pl.semaphore_wait(barrier, len(others))
 
     ex = R["ex_sem"]
     far_i = remote(inputs, R["far_i"], ex.at[0], ex.at[1], far)
@@ -135,6 +138,17 @@
     far_i.start()
     far_v.start()
     gv[...] = jnp.zeros_like(gv)
+    V = seg_v.shape[2]
+    across = lax.broadcasted_iota(jnp.int32, (T, T), 1)
+    down = lax.broadcasted_iota(jnp.int32, (T, T), 0)
+    wide_across = lax.broadcasted_iota(jnp.int32, (T, V), 1)
+    wide_down = lax.broadcasted_iota(jnp.int32, (T, V), 0)
+    spread = (wide_across // (V // T) == wide_down).astype(f32)
+    for r in range(B):
+        ids = segments[r : r + 1].astype(f32)
+        column = jnp.sum(jnp.where(across == down, ids, 0.0), axis=1, keepdims=True)
+        seg_q[r] = column
+        seg_v[r] = jnp.sum(spread * column, axis=0, keepdims=True)
     pick = [[(partner[r] == j).astype(f32) for j in range(B)] for r in range(B)]
     mix = [mixing[r] for r in range(B)]
 
@@ -234,7 +248,7 @@
         gv[shift : shift + 1] += column_sum(grad)
 
     def self_attend(r, qkv, weights, attended):
-        allowed = seg_q[r] == seg_k[r]
+        allowed = seg_q[r] == segments[pl.ds(r, 1)].astype(f32)
         for p in range(pairs):
             c = cols(p, PAIR)
             k = slice(D + c.start, D + c.stop)
@@ -254,6 +268,20 @@
             dqkv[r, :, c] = dq.astype(bf16)
             dqkv[r, :, k] = dk.astype(bf16)
             dqkv[r, :, v] = dv.astype(bf16)
+
+    def core_send(b):
+        rows = pl.ds(pl.multiple_of((1 - core) * half, half), half)
+        return remote(G.at[b, rows], R["core_in"].at[b], *sems(0, b), beside)
+
+    def sems(kind, b):
+        return R["r_send"].at[kind, b], R["r_recv"].at[kind, b]
+
+    half = D // 2
+
+    def produce(b, value):
+        G[b] = value.astype(bf16)
+        if fused:
+            core_send(b).start()
 
     n1, u1, s1, p1, a1 = R["n1"], R["u1"], R["s1"], R["p1"], R["a1"]
     qkv1, dqkv1, do1 = R["qkv1"], R["dqkv1"], R["do1"]
@@ -297,11 +325,14 @@
             gv[5:6] += column_sum(dqkv1[r, :, cols(0)])
 
         each_row(backward)
-        G[3] = t_dot(flat(a1), flat(gin)).astype(bf16)
         for b in range(3):
-            G[b] = t_dot(flat(n1), dqkv1[:, :, cols(b)].reshape(B * T, D)).astype(bf16)
-        for b in range(4, 8):
-            G[b] = jnp.zeros_like(G[b])
+            produce(b, t_dot(flat(n1), dqkv1[:, :, cols(b)].reshape(B * T, D)))
+        produce(3, t_dot(flat(a1), flat(gin)))
+        if fused:
+            w[1] = jnp.zeros(w.shape[1:], bf16)
+        else:
+            for b in range(4, 8):
+                G[b] = jnp.zeros((D, D), bf16)
 
     def feed_hidden(n, c):
         a = dot(n, w[0, :, cols(c)]) + vec[2 + c : 3 + c]
@@ -310,8 +341,8 @@
     def feed_grads(e_rows):
         def one(c, _):
             cc = pl.ds(pl.multiple_of(c * D, D), D)
-            G[4 + c] = t_dot(flat(e_rows), g[:, :, cc].reshape(B * T, D)).astype(bf16)
-            G[c] = t_dot(flat(n1), da[:, :, cc].reshape(B * T, D)).astype(bf16)
+            produce(4 + c, t_dot(flat(e_rows), g[:, :, cc].reshape(B * T, D)))
+            produce(c, t_dot(flat(n1), da[:, :, cc].reshape(B * T, D)))
             return 0
 
         lax.fori_loop(0, 4, one, 0)
@@ -466,16 +497,15 @@
             R["dw"][r] = dot_t(dkv2[r], w[0, :, D : 3 * D]).astype(bf16)
 
         each_row(source_grad)
-        G[7] = t_dot(flat(a1), flat(gin)).astype(bf16)
-        for b in range(3):
-            G[4 + b] = t_dot(flat(n1), dqkv1[:, :, cols(b)].reshape(B * T, D)).astype(bf16)
-        G[3] = t_dot(flat(a2), flat(dm)).astype(bf16)
-        G[0] = t_dot(flat(n2), flat(dq2)).astype(bf16)
+        produce(0, t_dot(flat(n2), flat(dq2)))
         for b in range(2):
             wide = view.shape[1]
-            G[1 + b] = t_dot(
-                view[...].reshape(B * wide, D), dkv2[:, :, cols(b)].reshape(B * wide, D)
-            ).astype(bf16)
+            grads = dkv2[:, :, cols(b)].reshape(B * wide, D)
+            produce(1 + b, t_dot(view[...].reshape(B * wide, D), grads))
+        produce(3, t_dot(flat(a2), flat(dm)))
+        for b in range(3):
+            produce(4 + b, t_dot(flat(n1), dqkv1[:, :, cols(b)].reshape(B * T, D)))
+        produce(7, t_dot(flat(a1), flat(gin)))
 
     part_i, part_v = R["part_i"], R["part_v"]
 
@@ -509,35 +539,161 @@
             scatter_v(k).start()
         part_v[...] = R["dw"][:, 2 * VS : 3 * VS]
 
-    @pl.when(z != 0)
-    def _():
-        scatter_i(0).wait_recv()
-
-    @pl.when(z != 2)
-    def _():
-        scatter_v(0).wait_recv()
-
-    owed_i, owed_v = R["owed_i"], R["owed_v"]
-    back = []
-    for part, owed, arrive, s in (
-        (part_i, owed_i, R["arr_i"], 4),
-        (part_v, owed_v, R["arr_v"], 6),
-    ):
-        for t in range(B):
-            owed[t] = sum(
-                pick[r][t] * (1.0 - mix[r]) * part[r].astype(f32) for r in range(B)
-            ).astype(bf16)
-        copy = remote(owed, arrive, ex.at[s], ex.at[s + 1], far)
-        copy.start()
-        back.append(copy)
-    for copy, part, arrive, out in (
-        (back[0], part_i, R["arr_i"], in_grad),
-        (back[1], part_v, R["arr_v"], view_grad),
-    ):
-        copy.wait_recv()
-        for r in range(B):
-            out[r] = (mix[r] * part[r].astype(f32) + arrive[r].astype(f32)).astype(bf16)
-        copy.wait_send()
+    def mixup_back():
+        @pl.when(z != 0)
+        def _():
+            scatter_i(0).wait_recv()
+
+        @pl.when(z != 2)
+        def _():
+            scatter_v(0).wait_recv()
+
+        owed_i, owed_v = R["owed_i"], R["owed_v"]
+        back = []
+        for part, owed, arrive, s in (
+            (part_i, owed_i, R["arr_i"], 4),
+            (part_v, owed_v, R["arr_v"], 6),
+        ):
+            for t in range(B):
+                owed[t] = sum(
+                    pick[r][t] * (1.0 - mix[r]) * part[r].astype(f32) for r in range(B)
+                ).astype(bf16)
+            copy = remote(owed, arrive, ex.at[s], ex.at[s + 1], far)
+            copy.start()
+            back.append(copy)
+        for copy, part, arrive, out in (
+            (back[0], part_i, R["arr_i"], in_grad),
+            (back[1], part_v, R["arr_v"], view_grad),
+        ):
+            copy.wait_recv()
+            for r in range(B):
+                out[r] = (mix[r] * part[r].astype(f32) + arrive[r].astype(f32)).astype(bf16)
+            copy.wait_send()
+
+    rx, ry, rx2, ry2, core_in = (R[k] for k in ("rx", "ry", "rx2", "ry2", "core_in"))
+    quarter, eighth = half // 4, half // 8
+    own = core * half
+    a0, b0 = own, own + half // 2
+    a_own, a_far = a0 + x_bit * quarter, a0 + (1 - x_bit) * quarter
+    b_own, b_far = b0 + y_bit * quarter, b0 + (1 - y_bit) * quarter
+    a_end, a_out = a_own + y_bit * eighth, a_own + (1 - y_bit) * eighth
+    b_end, b_out = b_own + x_bit * eighth, b_own + (1 - x_bit) * eighth
+    blocks = jnp.where(z == 0, 4, 8)
+
+    def part(start, length):
+        return pl.ds(pl.multiple_of(start, eighth), length)
+
+    def final(b, start, length):
+        return w.at[b // 4, part(start, length), pl.ds(pl.multiple_of(lax.rem(b, 4) * D, D), D)]
+
+    def scatter_x(b):
+        return remote(G.at[b, part(a_far, quarter)], rx.at[b], *sems(1, b), x_next)
+
+    def scatter_y(b):
+        return remote(G.at[b, part(b_far, quarter)], ry.at[b], *sems(2, b), far)
+
+    def scatter_xy(b):
+        return remote(G.at[b, part(a_out, eighth)], ry2.at[b], *sems(3, b), far)
+
+    def scatter_yx(b):
+        return remote(G.at[b, part(b_out, eighth)], rx2.at[b], *sems(4, b), x_next)
+
+    def spread_y(b):
+        return remote(final(b, a_end, eighth), final(b, a_end, eighth), *sems(5, b), far)
+
+    def spread_x(b):
+        return remote(final(b, b_end, eighth), final(b, b_end, eighth), *sems(6, b), x_next)
+
+    def spread_yx(b):
+        return remote(final(b, a_own, quarter), final(b, a_own, quarter), *sems(7, b), x_next)
+
+    def spread_xy(b):
+        return remote(final(b, b_own, quarter), final(b, b_own, quarter), *sems(8, b), far)
+
+    def spread_core(b):
+        return remote(final(b, own, half), final(b, own, half), *sems(9, b), beside)
+
+    def add(b, start, length, arrived):
+        rows = part(start, length)
+        G[b, rows] = (G[b, rows].astype(f32) + arrived[b].astype(f32)).astype(bf16)
+
+    def finish(b, start, arrived):
+        rows = part(start, eighth)
+        total = (G[b, rows].astype(f32) + arrived[b].astype(f32)).astype(bf16)
+        w[b // 4, rows, pl.ds(pl.multiple_of(lax.rem(b, 4) * D, D), D)] = total
+
+    def sum_core(b):
+        core_send(b).wait_recv()
+        add(b, own, half, core_in)
+        scatter_x(b).start()
+        scatter_y(b).start()
+
+    def sum_first(b):
+        scatter_x(b).wait_recv()
+        add(b, a_own, quarter, rx)
+        scatter_xy(b).start()
+        scatter_y(b).wait_recv()
+        add(b, b_own, quarter, ry)
+        scatter_yx(b).start()
+
+    def sum_second(b):
+        scatter_xy(b).wait_recv()
+        finish(b, a_end, ry2)
+        spread_y(b).start()
+        scatter_yx(b).wait_recv()
+        finish(b, b_end, rx2)
+        spread_x(b).start()
+
+    def pass_on(b):
+        spread_y(b).wait_recv()
+        spread_yx(b).start()
+        spread_x(b).wait_recv()
+        spread_xy(b).start()
+
+    def pass_core(b):
+        spread_yx(b).wait_recv()
+        spread_xy(b).wait_recv()
+        spread_core(b).start()
+
+    def arrive(b):
+        spread_core(b).wait_recv()
+
+    def sent(b):
+        for copy in (core_send, scatter_x, scatter_y, scatter_xy, scatter_yx, spread_y):
+            copy(b).wait_send()
+        for copy in (spread_x, spread_yx, spread_xy, spread_core):
+            copy(b).wait_send()
+
+    def vector_round(k, device):
+        return remote(gv, R["gv_in"].at[k], R["v_send"].at[k], R["v_recv"].at[k], device)
+
+    def vector_sum(k, device):
+        copy = vector_round(k, device)
+        copy.wait()
+        gv[...] += R["gv_in"][k]
+
+    def each_block(step):
+        lax.fori_loop(0, blocks, lambda b, c: (step(b), c)[1], 0)
+
+    if fused:
+        vector_round(0, beside).start()
+        each_block(sum_core)
+        vector_sum(0, beside)
+        vector_round(1, x_next).start()
+        each_block(sum_first)
+        vector_sum(1, x_next)
+        vector_round(2, far).start()
+        each_block(sum_second)
+        vector_sum(2, far)
+        each_block(pass_on)
+        mixup_back()
+        each_block(pass_core)
+        each_block(arrive)
+        each_block(sent)
+    else:
+        mixup_back()
+        for b in range(8):
+            w[b // 4, :, cols(b % 4)] = G[b]
 
     @pl.when(z == 0)
     def _():
@@ -583,17 +739,15 @@
         "vec": (vectors[0], vmem),
         "mixing": (mixing, smem),
         "partner": (partner, smem),
-        "seg_q": (segments[:, :, None], vmem),
-        "seg_k": (segments[:, None, :], vmem),
-        "seg_v": (jnp.repeat(segments, V // T, axis=1)[:, None, :], vmem),
+        "segments": (segments, vmem),
         "cot": (cotangent, vmem),
     }
     outs = {
         "records": (B, T, D, bf16),
         "in_grad": (B, TS, D, bf16),
         "view_grad": (B, VS, D, bf16),
-        "G": (8, D, D, bf16),
         "gv": (8, D, f32),
+        "w": (2, D, H, bf16),
     }
     dma = pltpu.SemaphoreType.DMA
 
@@ -601,7 +755,15 @@
         return pltpu.VMEM(shape, dtype)
 
     scratch = {
-        "w": buf(2, D, H),
+        "G": buf(8, D, D),
+        "core_in": buf(8, D // 2, D),
+        "rx": buf(8, D // 8, D),
+        "ry": buf(8, D // 8, D),
+        "rx2": buf(8, D // 16, D),
+        "ry2": buf(8, D // 16, D),
+        "gv_in": buf(3, 8, D, dtype=f32),
+        "seg_q": buf(B, T, 1, dtype=f32),
+        "seg_v": buf(B, 1, V, dtype=f32),
         "hin": buf(B, T, D),
         "gin": buf(B, T, D),
         "gout": buf(B, T, D),
@@ -652,23 +814,45 @@
         "si_send": dma((S,)),
         "sv_send": dma((S,)),
         "s_recv": dma((2,)),
+        "r_send": dma((10, 8)),
+        "r_recv": dma((10, 8)),
+        "v_send": dma((3,)),
+        "v_recv": dma((3,)),
     }
     names = list(args) + list(outs) + list(scratch)
-    records, in_grad, view_grad, G, gv = pl.pallas_call(
-        partial(kernel, names),
-        out_shape=[jax.ShapeDtypeStruct(s[:-1], s[-1]) for s in outs.values()],
+    fused = lax.axis_size("dp") == 8
+    records, in_grad, view_grad, gv, total = pl.pallas_call(
+        partial(kernel, names, fused),
+        out_shape=[
+            pltpu.VMEM(s[:-1], s[-1]) if k == "w" else jax.ShapeDtypeStruct(s[:-1], s[-1])
+            for k, s in outs.items()
+        ],
         in_specs=[spec for _, spec in args.values()],
         out_specs=[vmem] * len(outs),
         scratch_shapes=list(scratch.values()),
         compiler_params=pltpu.CompilerParams(
-            collective_id=0, has_side_effects=True, vmem_limit_bytes=60 << 20
+            collective_id=0, has_side_effects=True, vmem_limit_bytes=50 << 20
         ),
         name="relay",
     )(*[value for value, _ in args.values()])
-    total = lax.psum(G, "dp").astype(f32)
-    total = total.reshape(2, 4, D, D).transpose(0, 2, 1, 3).reshape(mats.shape)
-    summed = lax.psum(gv[: vectors.shape[1]], "dp")
-    return records[None], in_grad, view_grad, total, summed[None]
+    gv = gv[: vectors.shape[1]]
+    if not fused:
+        total, gv = lax.psum((total, gv), "dp")
+    wide = pl.pallas_call(
+        widen,
+        grid=(2, H // D),
+        out_shape=jax.ShapeDtypeStruct(mats.shape, f32),
+        in_specs=[vmem],
+        out_specs=pl.BlockSpec((1, 1, D, D), lambda t, c: (0, t, 0, c)),
+        compiler_params=pltpu.CompilerParams(vmem_limit_bytes=24 << 20),
+        name="widen",
+    )(total)
+    return records[None], in_grad, view_grad, wide, gv[None]
+
+
+def widen(total, wide):
+    t, c, D = pl.program_id(0), pl.program_id(1), wide.shape[2]
+    wide[0, 0] = total[t, :, pl.ds(pl.multiple_of(c * D, D), D)].astype(f32)
 
 
 def solution(mesh):

time: 303 us -> 187 us (0.62)
  waiting for transfers between devices: 120 us -> 0 us
  Pallas kernels: 87.4 us -> 181 us
  local copies, waits for them, and re-layouts: 36.9 us -> 4.79 us
  blocking collectives: 29.9 us -> 0 us
  between operations: 14.1 us -> 0.65 us
  other arithmetic: 12.7 us -> 0 us
    psum x1 -> x0, waiting for transfers between devices: 119 us -> none  [on_device(): total = lax.psum(G, 'dp').astype(f32)]
    pallas_call x1 -> x2, Pallas kernels: 87.4 us -> 181 us  [the longest x1 174 us: on_device(): pl.pallas_call(partial(kernel, names, fused), out_shape=[pltpu.VMEM(s[:-1...]
    psum x1 -> x0, blocking collectives: 29.9 us -> none  [on_device(): summed = lax.psum(gv[:vectors.shape[1]], 'dp')]
    reshape x1 -> x0, local copies, waits for them, and re-layouts: 16.9 us -> none  [on_device(): total = total.reshape(2, 4, D, D).transpose(0, 2, 1, 3).reshape(mats.shape)]
    reshape x1 -> x0, other arithmetic: 12.7 us -> none  [on_device(): total = total.reshape(2, 4, D, D).transpose(0, 2, 1, 3).reshape(mats.shape)]
    transpose x1 -> x0, local copies, waits for them, and re-layouts: 12.3 us -> none  [on_device(): total = total.reshape(2, 4, D, D).transpose(0, 2, 1, 3).reshape(mats.shape)]
  transfers between devices with their start and end apart: 1 -> 0, of which waited for: 1 -> 0; matrix products, arithmetic and copies ran while one was open for 0% -> 0% of each run, Pallas kernels for 0% -> 0%
where the time goes in v2:
time: 187 us
  Pallas kernels  181 us (97%)
  local copies, waits for them, and re-layouts  4.79 us (3%)
    pallas_call x1, Pallas kernels, on_device(): pl.pallas_call(partial(kernel, names, fused), out_shape=[pltpu.VMEM(s[:-1...  174 us
    pallas_call x1, Pallas kernels, on_device(): pl.pallas_call(widen, grid=(2, H // D), out_shape=jax.ShapeDtypeStruct(ma...  7 us
    unnamed x11, local copies, waits for them, and re-layouts  4.05 us

profile of v2, /device:TPU:9, one launch (start us, length us, event | category | flops | bytes accessed | tf_op | source)
XLA Modules:
  0.0 186.8 jit_solution(4969118183146619519)
XLA Ops:
  0.6 1.3 copy.16
  2.0 174.3 %relay.1 = (bf16[2,128,768]{2,1,0:T(8,128)(2,1)}, bf16[2,32,768]{2,1,0:T(8,128)(2,1)}, bf16[2,64,768]{2,1,0:T(8,128)(2,1)}, f32[8,768]{1,0:T(8,128)}, bf16[2,768,3072]{2,1,0:T(8,128)(2,1)S(1)}) custom-call(bf16[2,32,768]{2,1,0:T(8,128)(2,1)} %refs_0_.1, bf16[2,64,768]{2,1,0:T(8,128)(2,1)} %refs_1_.1, bf16[1,2,768,3072]{3,2,1,0:T(8,128)(2,1)} %refs_2_.1, ...), custom_call_target="tpu_custom_call" | custom-call | tf_op jit(solution)/shard_map/relay/pallas_call | solution.py:824
  176.3 0.7 slice_bitcast_fusion
  177.0 0.6 copy.13
  177.7 0.0 copy-start
  177.7 0.0 copy-start.2
  177.7 0.0 copy-start.1
  177.7 7.0 %widen.1 = f32[1,2,768,3072]{3,2,1,0:T(8,128)} custom-call(bf16[2,768,3072]{2,1,0:T(8,128)(2,1)S(1)} %get-tuple-element.13.total), custom_call_target="tpu_custom_call" | custom-call | tf_op jit(solution)/shard_map/widen/pallas_call | solution.py:841
  184.7 0.0 copy-done
  184.7 0.7 copy.20
  185.4 0.0 copy-done.2
  185.4 0.6 copy.21
  186.1 0.0 copy-done.1
  186.1 0.7 copy.22
Async XLA Ops:
  177.7 7.0 %copy-start = (bf16[2,128,768]{2,1,0:T(8,128)(2,1)S(1)}, bf16[2,128,768]{2,1,0:T(8,128)(2,1)}, u32[]{:S(2)}) copy-start(bf16[2,128,768]{2,1,0:T(8,128)(2,1)} %get-tuple-element.10) | copy-start | bytes 1179652
  177.7 7.8 %copy-start.2 = (bf16[2,32,768]{2,1,0:T(8,128)(2,1)S(1)}, bf16[2,32,768]{2,1,0:T(8,128)(2,1)}, u32[]{:S(2)}) copy-start(bf16[2,32,768]{2,1,0:T(8,128)(2,1)} %get-tuple-element.26) | copy-start | bytes 294916
  177.7 8.4 %copy-start.1 = (bf16[2,64,768]{2,1,0:T(8,128)(2,1)S(1)}, bf16[2,64,768]{2,1,0:T(8,128)(2,1)}, u32[]{:S(2)}) copy-start(bf16[2,64,768]{2,1,0:T(8,128)(2,1)} %get-tuple-element.27) | copy-start | bytes 589828

commit v3 on v2

v3 whole, which is shorter than its diff:
```python
from functools import partial

import jax
import jax.numpy as jnp
from jax import lax
from jax.experimental import pallas as pl
from jax.experimental.pallas import tpu as pltpu
from jax.sharding import PartitionSpec as P

HEAD = 64
PAIR = 2 * HEAD
MESH = pl.DeviceIdType.MESH
bf16 = jnp.bfloat16
f32 = jnp.float32


def dot(a, b):
    return lax.dot_general(a, b, (((1,), (0,)), ((), ())), preferred_element_type=f32)


def dot_t(a, b):
    return lax.dot_general(a, b, (((1,), (1,)), ((), ())), preferred_element_type=f32)


def t_dot(a, b):
    return lax.dot_general(a, b, (((0,), (0,)), ((), ())), preferred_element_type=f32)


def row_mean(x):
    return jnp.sum(x, axis=-1, keepdims=True) * (1.0 / x.shape[-1])


def normalize(h):
    center = h - row_mean(h)
    scale = lax.rsqrt(row_mean(center * center) + 1e-06)
    return center * scale, scale


def normalize_back(grad, unit, scale, gain):
    inner = grad * gain
    return scale * (inner - row_mean(inner) - unit * row_mean(inner * unit))


def gelu_parts(a):
    cdf = 0.5 * (1.0 + lax.erf(a * (0.5**0.5)))
    pdf = jnp.exp(a * a * (-0.5)) * 0.3989422804014327
    return a * cdf, cdf + a * pdf


def halves(x):
    low = lax.broadcasted_iota(jnp.int32, x.shape, 1) < HEAD
    zero = jnp.zeros_like(x)
    return jnp.concatenate([jnp.where(low, x, zero), jnp.where(low, zero, x)], axis=0)


def softmax(scores, allowed):
    scores = jnp.where(allowed, scores, -1000000000.0)
    weights = jnp.exp(scores - jnp.max(scores, axis=-1, keepdims=True))
    return weights * (1.0 / jnp.sum(weights, axis=-1, keepdims=True))


def attend_pair(q, k, v, allowed):
    n = k.shape[0]
    scores = dot_t(q, halves(k))
    weights = jnp.concatenate(
        [softmax(scores[:, :n], allowed), softmax(scores[:, n:], allowed)], axis=1
    )
    return dot(weights.astype(bf16), halves(v)), weights


def score_grads(v, weights, grad):
    n = v.shape[0]
    grad_weights = dot_t(grad, halves(v))
    product = weights * grad_weights
    parts = []
    for part in (slice(0, n), slice(n, 2 * n)):
        total = jnp.sum(product[:, part], axis=-1, keepdims=True)
        parts.append((product[:, part] - weights[:, part] * total).astype(bf16))
    return jnp.concatenate(parts, axis=1)


def query_grads(k, grad_scores):
    return dot(grad_scores, halves(k)) * (HEAD**-0.5)


def stacked(x):
    n = x.shape[1] // 2
    return jnp.concatenate([x[:, :n], x[:, n:]], axis=0)


def key_grads(q, weights, grad, grad_scores):
    grad_k = t_dot(stacked(grad_scores), halves(q))
    grad_v = t_dot(stacked(weights.astype(bf16)), halves(grad))
    return grad_k, grad_v


def column_sum(x):
    return jnp.sum(x.astype(f32), axis=0, keepdims=True)


def kernel(names, fused, *refs):
    R = dict(zip(names, refs))
    inputs, other_view, mats, vec = (R[k] for k in ("inputs", "other_view", "mats", "vec"))
    mixing, partner, cot = R["mixing"], R["partner"], R["gin"]
    segments, seg_q, seg_v = R["segments"], R["seg_q"], R["seg_v"]
    records, in_grad, view_grad = R["records"], R["in_grad"], R["view_grad"]
    G, gv, w = R["G"], R["gv"], R["w"]
    wt = G
    hin, gin, gout = R["hin"], R["gin"], R["gout"]
    B, TS, D = inputs.shape
    VS = other_view.shape[1]
    T = segments.shape[1]
    V = seg_v.shape[2]
    S = lax.axis_size("section")
    n_dp = lax.axis_size("dp")
    z = lax.axis_index("section")
    d = lax.axis_index("dp")
    far = {"dp": lax.rem(d + n_dp // 2, n_dp)}
    pairs = D // PAIR
    CH = T // 2
    chunks = B * 2
    core, x_bit, y_bit = lax.rem(d, 2), lax.rem(d // 2, 2), d // 4
    beside = {"dp": d + 1 - 2 * core}
    x_next = {"dp": d + 2 - 4 * x_bit}

    def remote(src, dst, send, recv, device):
        return pltpu.make_async_remote_copy(
            src_ref=src,
            dst_ref=dst,
            send_sem=send,
            recv_sem=recv,
            device_id=device,
            device_id_type=MESH,
        )

    def block_columns(b):
        return pl.ds(b * D, D)

    def table(b):
        return pltpu.make_async_copy(
            mats.at[0, b // 4, :, block_columns(b % 4)], w.at[b], R["w_sem"].at[b]
        )

    def local(src, dst, k):
        return pltpu.make_async_copy(src, dst, R["l_sem"].at[k])

    def at(i, length):
        return pl.ds(pl.multiple_of(i * length, length), length)

    own_i = local(inputs, R["own_i"], 0)
    own_v = local(other_view, R["own_v"], 1)
    own_cot = local(R["cot"], gin, 2)
    barrier = pltpu.get_barrier_semaphore()
    others = [far] + [{"section": lax.rem(z + o, S)} for o in range(1, S)]
    if fused:
        others += [beside, x_next]
    for other in others:
        pl.semaphore_signal(barrier, inc=1, device_id=other, device_id_type=MESH)
    own_i.start()
    own_v.start()
    for b in range(8):
        table(b).start()

    @pl.when(z == S - 1)
    def _():
        own_cot.start()

    gv[...] = jnp.zeros_like(gv)
    pick = [[(partner[r] == j).astype(f32) for j in range(B)] for r in range(B)]
    mix = [mixing[r] for r in range(B)]
    pl.semaphore_wait(barrier, len(others))

    ex = R["ex_sem"]
    far_i = remote(inputs, R["far_i"], ex.at[0], ex.at[1], far)
    far_v = remote(other_view, R["far_v"], ex.at[2], ex.at[3], far)
    far_i.start()

    @pl.when(z == 0)
    def _():
        far_v.start()

    across = lax.broadcasted_iota(jnp.int32, (T, T), 1)
    down = lax.broadcasted_iota(jnp.int32, (T, T), 0)
    wide_across = lax.broadcasted_iota(jnp.int32, (T, V), 1)
    wide_down = lax.broadcasted_iota(jnp.int32, (T, V), 0)
    spread = (wide_across // (V // T) == wide_down).astype(f32)
    for r in range(B):
        ids = segments[r : r + 1].astype(f32)
        column = jnp.sum(jnp.where(across == down, ids, 0.0), axis=1, keepdims=True)
        seg_q[r] = column
        seg_v[r] = jnp.sum(spread * column, axis=0, keepdims=True)

    def blend(own, other, r):
        chosen = sum(pick[r][j] * other[j].astype(f32) for j in range(B))
        return (mix[r] * own[r].astype(f32) + (1.0 - mix[r]) * chosen).astype(bf16)

    def gather_i(r, source):
        return remote(
            R["stage_i"].at[r],
            hin.at[pl.ds(pl.multiple_of(r * T + source * TS, TS), TS)],
            R["gi_send"].at[r],
            R["gi_recv"].at[r, source],
            {"section": 0},
        )

    def gather_v(r, source):
        return remote(
            R["stage_v"].at[r],
            R["view"].at[pl.ds(pl.multiple_of(r * V + source * VS, VS), VS)],
            R["gv_send"].at[r],
            R["gv_recv"].at[r, source],
            {"section": 2},
        )

    own_i.wait()
    far_i.wait_recv()
    for r in range(B):
        mixed = blend(R["own_i"], R["far_i"], r)

        @pl.when(z == 0)
        def _():
            hin[r * T : r * T + TS] = mixed

        @pl.when(z != 0)
        def _():
            R["stage_i"][r] = mixed
            gather_i(r, z).start()

    @pl.when(z != 0)
    def _():
        far_v.start()

    own_v.wait()
    far_v.wait_recv()
    for r in range(B):
        mixed_view = blend(R["own_v"], R["far_v"], r)

        @pl.when(z == 2)
        def _():
            R["view"][r * V + 2 * VS : r * V + 3 * VS] = mixed_view

        @pl.when(z != 2)
        def _():
            R["stage_v"][r] = mixed_view
            gather_v(r, z).start()

    far_i.wait_send()
    far_v.wait_send()

    def forward_hop(i):
        part = at(i, CH)
        return remote(
            records.at[part],
            hin.at[part],
            R["f_send"].at[i],
            R["f_recv"].at[i],
            {"section": z + 1},
        )

    def backward_hop(i):
        part = at(i, CH)
        return remote(
            gout.at[part], gin.at[part], R["b_send"].at[i], R["b_recv"].at[i], {"section": z - 1}
        )

    def entered(i):
        part = hin.at[at(i, CH)]
        remote(
            part, part, R["f_send"].at[i], R["f_recv"].at[i], {"section": z - 1}
        ).wait_recv()

    def returned(i):
        part = gin.at[at(i, CH)]
        remote(
            part, part, R["b_send"].at[i], R["b_recv"].at[i], {"section": z + 1}
        ).wait_recv()

    def both(step, r):
        step(2 * r)
        step(2 * r + 1)

    def forward_hops(r):
        forward_hop(2 * r).start()
        forward_hop(2 * r + 1).start()

    def backward_hops(r):
        backward_hop(2 * r).start()
        backward_hop(2 * r + 1).start()

    def each_row(step):
        lax.fori_loop(0, B, lambda r, c: (step(r), c)[1], 0)

    def each_chunk(step):
        lax.fori_loop(0, chunks, lambda i, c: (step(i), c)[1], 0)

    def cols(b, width=D):
        return slice(b * width, (b + 1) * width)

    def tables_ready():
        for b in range(8):
            table(b).wait()

    def turned(first, last):
        def one(b, c):
            wt[b] = jnp.transpose(w[b])
            return c

        lax.fori_loop(first, last, one, 0)

    def norm_in(h, rows, unit, scale, normed, gain, shift):
        unit_value, scale_value = normalize(h)
        unit[rows] = unit_value
        scale[rows] = scale_value
        value = (unit_value * vec[gain] + vec[shift]).astype(bf16)
        normed[rows] = value
        return value

    def norm_out(grad, rows, unit, scale, gain):
        return normalize_back(grad, unit[rows], scale[rows], vec[gain])

    def norm_sums(grad, unit, gain, shift):
        gv[gain : gain + 1] = column_sum(grad[...] * unit[...])
        gv[shift : shift + 1] = column_sum(grad[...])

    def key_columns(p, start):
        return slice(start + p * PAIR, start + (p + 1) * PAIR)

    def self_attend(r, rows, qkv, weights, attended):
        allowed = seg_q[r] == segments[pl.ds(r, 1)].astype(f32)
        for p in range(pairs):
            c, k, v = (key_columns(p, start) for start in (0, D, 2 * D))
            out, kept = attend_pair(qkv[rows, c], qkv[rows, k], qkv[rows, v], allowed)
            attended[rows, c] = out.astype(bf16)
            weights[r, p] = kept

    def self_attend_back(r, rows, qkv, weights, grad, dqkv):
        for p in range(pairs):
            c, k, v = (key_columns(p, start) for start in (0, D, 2 * D))
            kept, do = weights[r, p], grad[rows, c]
            ds = score_grads(qkv[rows, v], kept, do)
            dqkv[rows, c] = query_grads(qkv[rows, k], ds).astype(bf16)
            dk, dv = key_grads(qkv[rows, c], kept, do, ds)
            dqkv[rows, k] = dk.astype(bf16)
            dqkv[rows, v] = dv.astype(bf16)

    half = D // 2

    def sems(kind, b):
        return R["r_send"].at[kind, b], R["r_recv"].at[kind, b]

    def core_send(b):
        rows = pl.ds(pl.multiple_of((1 - core) * half, half), half)
        return remote(G.at[b, rows], R["core_in"].at[b], *sems(0, b), beside)

    def produce(b, value):
        G[b] = value.astype(bf16)
        if fused:
            core_send(b).start()

    def follow(b):
        if fused:
            sum_core(b)

    part_i, part_v = R["part_i"], R["part_v"]

    def part_copy_i(r, k):
        return remote(
            gout.at[pl.ds(pl.multiple_of(r * T + k * TS, TS), TS)],
            part_i.at[r],
            R["si_send"].at[r, k],
            R["si_recv"].at[r],
            {"section": k},
        )

    def part_copy_v(r, k):
        return remote(
            R["dw"].at[pl.ds(pl.multiple_of(r * V + k * VS, VS), VS)],
            part_v.at[r],
            R["sv_send"].at[r, k],
            R["sv_recv"].at[r],
            {"section": k},
        )

    def scatter_i(r):
        for k in range(1, S):
            part_copy_i(r, k).start()

    def scatter_v(r):
        for k in (0, 1, 3):
            part_copy_v(r, k).start()

    rx, ry, rx2, ry2, core_in = (R[k] for k in ("rx", "ry", "rx2", "ry2", "core_in"))
    quarter, eighth = half // 4, half // 8
    own = core * half
    a0, b0 = own, own + half // 2
    a_own, a_far = a0 + x_bit * quarter, a0 + (1 - x_bit) * quarter
    b_own, b_far = b0 + y_bit * quarter, b0 + (1 - y_bit) * quarter
    a_end, a_out = a_own + y_bit * eighth, a_own + (1 - y_bit) * eighth
    b_end, b_out = b_own + x_bit * eighth, b_own + (1 - x_bit) * eighth
    blocks = jnp.where(z == 0, 4, 8)
    shift = jnp.where(z == 2, 4, 0)

    def part(start, length):
        return pl.ds(pl.multiple_of(start, eighth), length)

    def final(b, start, length):
        return w.at[b, part(start, length)]

    def scatter_x(b):
        return remote(G.at[b, part(a_far, quarter)], rx.at[b], *sems(1, b), x_next)

    def scatter_y(b):
        return remote(G.at[b, part(b_far, quarter)], ry.at[b], *sems(2, b), far)

    def scatter_xy(b):
        return remote(G.at[b, part(a_out, eighth)], ry2.at[b], *sems(3, b), far)

    def scatter_yx(b):
        return remote(G.at[b, part(b_out, eighth)], rx2.at[b], *sems(4, b), x_next)

    def spread_y(b):
        return remote(final(b, a_end, eighth), final(b, a_end, eighth), *sems(5, b), far)

    def spread_x(b):
        return remote(final(b, b_end, eighth), final(b, b_end, eighth), *sems(6, b), x_next)

    def spread_yx(b):
        return remote(final(b, a_own, quarter), final(b, a_own, quarter), *sems(7, b), x_next)

    def spread_xy(b):
        return remote(final(b, b_own, quarter), final(b, b_own, quarter), *sems(8, b), far)

    def spread_core(b):
        return remote(final(b, own, half), final(b, own, half), *sems(9, b), beside)

    def add(b, start, length, arrived):
        rows = part(start, length)
        G[b, rows] = (G[b, rows].astype(f32) + arrived[b].astype(f32)).astype(bf16)

    def finish(b, start, arrived):
        rows = part(start, eighth)
        total = (G[b, rows].astype(f32) + arrived[b].astype(f32)).astype(bf16)
        w[b, rows] = total

    def sum_core(b):
        core_send(b).wait_recv()
        add(b, own, half, core_in)
        scatter_x(b).start()
        scatter_y(b).start()

    n1, u1, s1, p1, a1 = R["n1"], R["u1"], R["s1"], R["p1"], R["a1"]
    qkv1, dqkv1, do1, dn1 = R["qkv1"], R["dqkv1"], R["do1"], R["dn1"]
    n2, u2, s2, a2 = R["n2"], R["u2"], R["s2"], R["a2"]
    q2, dq2, kv2, dkv2, do2, dn2 = (R[k] for k in ("q2", "dq2", "kv2", "dkv2", "do2", "dn2"))
    view, dm = R["view"], R["dm"]
    g, gp, da = R["g"], R["gp"], R["da"]
    p2, ds2 = gp, da
    wide_pair = 2 * V
    SCALE = HEAD**-0.5

    def wide_t(first, count):
        return wt[first : first + count].reshape(count * D, D)

    @pl.when(z == 0)
    def _():
        tables_ready()

        def forward(r):
            rows = at(r, T)
            for k in range(1, S):
                gather_i(r, k).wait_recv()
            h = hin[rows].astype(f32)
            n = norm_in(h, rows, u1, s1, n1, 0, 1)
            q = (dot(n, w[0]) + vec[5]).astype(bf16)
            qkv1[rows, cols(0)] = q * SCALE
            qkv1[rows, cols(1)] = dot(n, w[1]).astype(bf16)
            qkv1[rows, cols(2)] = (dot(n, w[2]) + vec[2]).astype(bf16)
            self_attend(r, rows, qkv1, p1, a1)
            out = h + dot(a1[rows], w[3]) + vec[4]
            records[rows] = out.astype(bf16)
            forward_hops(r)

        each_row(forward)
        turned(0, 4)

        def backward(r):
            rows = at(r, T)
            both(returned, r)
            e = gin[rows]
            do1[rows] = dot(e, wt[3]).astype(bf16)
            self_attend_back(r, rows, qkv1, p1, do1, dqkv1)
            dn = dot(dqkv1[rows], wide_t(0, 3))
            dn1[rows] = dn
            gout[rows] = (e.astype(f32) + norm_out(dn, rows, u1, s1, 0)).astype(bf16)
            scatter_i(r)

        each_row(backward)
        for b in range(3):
            produce(b, t_dot(n1[...], dqkv1[:, cols(b)]))
        follow(0)
        produce(3, t_dot(a1[...], gin[...]))
        for b in range(1, 4):
            follow(b)
        norm_sums(dn1, u1, 0, 1)
        gv[2:3] = column_sum(dqkv1[:, cols(2)])
        gv[4:5] = column_sum(gin[...])
        gv[5:6] = column_sum(dqkv1[:, cols(0)])
        for r in range(B):
            part_i[r] = gout[r * T : r * T + TS]
        if fused:
            for b in range(4, 8):
                w[b] = jnp.zeros((D, D), bf16)
        else:
            for b in range(4, 8):
                G[b] = jnp.zeros((D, D), bf16)

    def feed_hidden(n, c):
        a = dot(n, w[c]) + vec[2 + c]
        return gelu_parts(a)

    def feed_grads(first, last, left, right, start):
        def one(c, _):
            produce(first + c, t_dot(left[...], right[:, at(c, D)]))
            pl.when(first + c >= 2)(lambda: follow(first + c - 2))
            return 0

        lax.fori_loop(0, last - first, one, 0)

    def feed_sums():
        norm_sums(dn1, u1, 0, 1)
        for c in range(4):
            gv[2 + c : 3 + c] = column_sum(da[:, cols(c)])
        gv[6:7] = column_sum(gin[...])

    @pl.when(z == 1)
    def _():
        tables_ready()
        turned(0, 8)

        def forward(i):
            rows = at(i, CH)
            entered(i)
            h = hin[rows].astype(f32)
            n = norm_in(h, rows, u1, s1, n1, 0, 1)
            out = h + vec[6]
            for c in range(4):
                active, slope = feed_hidden(n, c)
                active = active.astype(bf16)
                g[rows, cols(c)] = active
                gp[rows, cols(c)] = slope
                out += dot(active, wt[4 + c])
            records[rows] = out.astype(bf16)
            forward_hop(i).start()

        each_chunk(forward)

        def backward(i):
            rows = at(i, CH)
            returned(i)
            e = gin[rows]
            dn = jnp.zeros((CH, D), f32)
            for c in range(4):
                dg = dot(e, w[4 + c])
                dc = (dg * gp[rows, cols(c)]).astype(bf16)
                da[rows, cols(c)] = dc
                dn += dot(dc, wt[c])
            dn1[rows] = dn
            gout[rows] = (e.astype(f32) + norm_out(dn, rows, u1, s1, 0)).astype(bf16)
            backward_hop(i).start()

        each_chunk(backward)
        feed_grads(0, 4, n1, da, 0)
        feed_grads(4, 8, gin, g, 4)
        follow(6)
        follow(7)
        feed_sums()

    @pl.when(z == 3)
    def _():
        tables_ready()
        turned(0, 4)
        own_cot.wait()

        def ahead(r):
            rows = at(r, T)
            e = cot[rows]
            for c in range(4):
                gp[rows, cols(c)] = dot(e, w[4 + c])

        each_row(ahead)

        def turn(i):
            rows = at(i, CH)
            entered(i)
            e = cot[rows]
            n = norm_in(hin[rows].astype(f32), rows, u1, s1, n1, 0, 1)
            dn = jnp.zeros((CH, D), f32)
            for c in range(4):
                active, slope = feed_hidden(n, c)
                g[rows, cols(c)] = active.astype(bf16)
                dc = (gp[rows, cols(c)] * slope).astype(bf16)
                da[rows, cols(c)] = dc
                dn += dot(dc, wt[c])
            dn1[rows] = dn
            gout[rows] = (e.astype(f32) + norm_out(dn, rows, u1, s1, 0)).astype(bf16)
            backward_hop(i).start()

        each_chunk(turn)
        feed_grads(0, 4, n1, da, 0)

        def output(r):
            rows = at(r, T)
            out = hin[rows].astype(f32) + vec[6]
            for c in range(4):
                out += dot_t(g[rows, cols(c)], w[4 + c])
            records[rows] = out.astype(bf16)

        each_row(output)
        feed_grads(4, 8, cot, g, 4)
        follow(6)
        follow(7)
        feed_sums()

    @pl.when(z == 2)
    def _():
        tables_ready()

        def ahead(r):
            wide = at(r, V)
            for k in (0, 1, 3):
                gather_v(r, k).wait_recv()
            for b in range(2):
                kv2[wide, cols(b)] = dot(view[wide], w[1 + b]).astype(bf16)

        each_row(ahead)
        turned(3, 8)
        wt[0] = jnp.transpose(w[0])

        def forward(r):
            rows, wide = at(r, T), at(r, V)
            both(entered, r)
            h = hin[rows].astype(f32)
            n = norm_in(h, rows, u2, s2, n2, 0, 1)
            q2[rows] = dot(n, w[0]).astype(bf16) * SCALE
            allowed = seg_q[r] == seg_v[r]
            for p in range(pairs):
                c, v = (key_columns(p, start) for start in (0, D))
                out, kept = attend_pair(q2[rows, c], kv2[wide, c], kv2[wide, v], allowed)
                a2[rows, c] = out.astype(bf16)
                p2[rows, cols(p, wide_pair)] = kept
            m = h + dot(a2[rows], w[3]) + vec[4]
            n = norm_in(m, rows, u1, s1, n1, 2, 3)
            q = (dot(n, w[4]) + vec[5]).astype(bf16)
            qkv1[rows, cols(0)] = q * SCALE
            qkv1[rows, cols(1)] = dot(n, w[5]).astype(bf16)
            qkv1[rows, cols(2)] = dot(n, w[6]).astype(bf16)
            self_attend(r, rows, qkv1, p1, a1)
            out = m + dot(a1[rows], w[7]) + vec[6]
            records[rows] = out.astype(bf16)
            forward_hops(r)

        each_row(forward)

        def backward(r):
            rows, wide = at(r, T), at(r, V)
            both(returned, r)
            e = gin[rows]
            do1[rows] = dot(e, wt[7]).astype(bf16)
            self_attend_back(r, rows, qkv1, p1, do1, dqkv1)
            dn = dot(dqkv1[rows], wide_t(4, 3))
            dn1[rows] = dn
            dmid = e.astype(f32) + norm_out(dn, rows, u1, s1, 2)
            dm[rows] = dmid
            do2[rows] = dot(dmid.astype(bf16), wt[3]).astype(bf16)
            for p in range(pairs):
                c, v = (key_columns(p, start) for start in (0, D))
                ds = score_grads(kv2[wide, v], p2[rows, cols(p, wide_pair)], do2[rows, c])
                ds2[rows, cols(p, wide_pair)] = ds
                dq2[rows, c] = query_grads(kv2[wide, c], ds).astype(bf16)
            dn = dot(dq2[rows], wt[0])
            dn2[rows] = dn
            gout[rows] = (dmid + norm_out(dn, rows, u2, s2, 0)).astype(bf16)
            backward_hops(r)

        each_row(backward)
        for b in range(3):
            produce(4 + b, t_dot(n1[...], dqkv1[:, cols(b)]))
        follow(4)
        produce(7, t_dot(a1[...], gin[...]))
        follow(5)

        def source_grad(r):
            rows, wide = at(r, T), at(r, V)
            for p in range(pairs):
                c, v = (key_columns(p, start) for start in (0, D))
                x = cols(p, wide_pair)
                dk, dv = key_grads(q2[rows, c], p2[rows, x], do2[rows, c], ds2[rows, x])
                dkv2[wide, c] = dk.astype(bf16)
                dkv2[wide, v] = dv.astype(bf16)
            dw = dot_t(dkv2[wide, cols(0)], w[1]) + dot_t(dkv2[wide, cols(1)], w[2])
            R["dw"][wide] = dw.astype(bf16)
            scatter_v(r)

        each_row(source_grad)
        for b in range(2):
            produce(b, t_dot(n2[...], dq2[...]) if b == 0 else t_dot(view[...], dkv2[:, cols(0)]))
            follow(6 + b)
        produce(2, t_dot(view[...], dkv2[:, cols(1)]))
        follow(0)
        produce(3, t_dot(a2[...], dm[...].astype(bf16)))
        for b in range(1, 4):
            follow(b)
        norm_sums(dn1, u1, 2, 3)
        norm_sums(dn2, u2, 0, 1)
        gv[4:5] = column_sum(dm[...])
        gv[5:6] = column_sum(dqkv1[:, cols(0)])
        gv[6:7] = column_sum(gin[...])
        for r in range(B):
            part_v[r] = R["dw"][r * V + 2 * VS : r * V + 3 * VS]

    owed_i, owed_v = R["owed_i"], R["owed_v"]
    owed_to = [
        remote(owed_i, R["arr_i"], ex.at[4], ex.at[5], far),
        remote(owed_v, R["arr_v"], ex.at[6], ex.at[7], far),
    ]

    def mixup_back():
        @pl.when(z != 0)
        def _():
            for r in range(B):
                part_copy_i(r, 0).wait_recv()

        @pl.when(z != 2)
        def _():
            for r in range(B):
                part_copy_v(r, 0).wait_recv()

        for part, owed, copy in zip((part_i, part_v), (owed_i, owed_v), owed_to):
            for t in range(B):
                owed[t] = sum(
                    pick[r][t] * (1.0 - mix[r]) * part[r].astype(f32) for r in range(B)
                ).astype(bf16)
            copy.start()

    def mixup_end():
        for part, arrived, out, copy in zip(
            (part_i, part_v), (R["arr_i"], R["arr_v"]), (in_grad, view_grad), owed_to
        ):
            copy.wait_recv()
            for r in range(B):
                out[r] = (mix[r] * part[r].astype(f32) + arrived[r].astype(f32)).astype(bf16)
            copy.wait_send()

    def sum_first(b):
        scatter_x(b).wait_recv()
        add(b, a_own, quarter, rx)
        scatter_xy(b).start()
        scatter_y(b).wait_recv()
        add(b, b_own, quarter, ry)
        scatter_yx(b).start()

    def sum_second(b):
        scatter_xy(b).wait_recv()
        finish(b, a_end, ry2)
        spread_y(b).start()
        scatter_yx(b).wait_recv()
        finish(b, b_end, rx2)
        spread_x(b).start()

    def pass_on(b):
        spread_y(b).wait_recv()
        spread_yx(b).start()
        spread_x(b).wait_recv()
        spread_xy(b).start()

    def pass_core(b):
        spread_yx(b).wait_recv()
        spread_xy(b).wait_recv()
        spread_core(b).start()

    def arrive(b):
        spread_core(b).wait_recv()

    def sent(b):
        for copy in (core_send, scatter_x, scatter_y, scatter_xy, scatter_yx, spread_y):
            copy(b).wait_send()
        for copy in (spread_x, spread_yx, spread_xy, spread_core):
            copy(b).wait_send()

    def vector_round(k, device):
        return remote(gv, R["gv_in"].at[k], R["v_send"].at[k], R["v_recv"].at[k], device)

    def vector_sum(k, device):
        copy = vector_round(k, device)
        copy.wait()
        gv[...] += R["gv_in"][k]

    def each_block(step):
        lax.fori_loop(0, blocks, lambda i, c: (step(lax.rem(i + shift, 8)), c)[1], 0)

    if fused:
        vector_round(0, beside).start()
        vector_sum(0, beside)
        vector_round(1, x_next).start()
        each_block(sum_first)
        vector_sum(1, x_next)
        vector_round(2, far).start()
        each_block(sum_second)
        vector_sum(2, far)
        mixup_back()
        each_block(pass_on)
        each_block(pass_core)
        each_block(arrive)
        mixup_end()
        each_block(sent)
    else:
        mixup_back()
        mixup_end()
        for b in range(8):
            w[b] = G[b]

    for i in range(vec.shape[0]):
        R["gv_out"][i] = gv[i : i + 1]

    @pl.when(z == 0)
    def _():
        for r in range(B):
            for k in range(1, S):
                part_copy_i(r, k).wait_send()

    @pl.when(z == 2)
    def _():
        for r in range(B):
            for k in (0, 1, 3):
                part_copy_v(r, k).wait_send()

    for r in range(B):

        @pl.when(z != 0)
        def _():
            gather_i(r, z).wait_send()

        @pl.when(z != 2)
        def _():
            gather_v(r, z).wait_send()

    for i in range(chunks):

        @pl.when(z != 0)
        def _():
            backward_hop(i).wait_send()

        @pl.when(z != S - 1)
        def _():
            forward_hop(i).wait_send()


def on_device(inputs, other_view, mats, vectors, mixing, partner, segments, cotangent):
    B, TS, D = inputs.shape
    VS = other_view.shape[1]
    T = segments.shape[1]
    S = lax.axis_size("section")
    V = VS * S
    H = mats.shape[3]
    pairs = D // PAIR
    vmem = pl.BlockSpec(memory_space=pltpu.VMEM)
    smem = pl.BlockSpec(memory_space=pltpu.SMEM)
    hbm = pl.BlockSpec(memory_space=pl.ANY)
    args = {
        "inputs": (inputs, hbm),
        "other_view": (other_view, hbm),
        "mats": (mats, hbm),
        "vec": (jnp.swapaxes(vectors, 0, 1), vmem),
        "mixing": (mixing, smem),
        "partner": (partner, smem),
        "segments": (segments, vmem),
        "cot": (cotangent.reshape(B * T, D), hbm),
    }
    outs = {
        "records": (B * T, D, bf16),
        "in_grad": (B, TS, D, bf16),
        "view_grad": (B, VS, D, bf16),
        "gv_out": (vectors.shape[1], 1, D, f32),
        "w": (8, D, D, bf16),
    }
    dma = pltpu.SemaphoreType.DMA

    def buf(*shape, dtype=bf16):
        return pltpu.VMEM(shape, dtype)

    scratch = {"G": buf(8, D, D), "core_in": buf(8, D // 2, D)}
    scratch |= {k: buf(8, D // 8, D) for k in ("rx", "ry")}
    scratch |= {k: buf(8, D // 16, D) for k in ("rx2", "ry2")}
    scratch |= {"gv": buf(8, D, dtype=f32), "gv_in": buf(3, 8, D, dtype=f32)}
    scratch |= {"seg_q": buf(B, T, 1, dtype=f32), "seg_v": buf(B, 1, V, dtype=f32)}
    for k in ("own", "far", "stage", "part", "owed", "arr"):
        scratch |= {k + "_i": buf(B, TS, D), k + "_v": buf(B, VS, D)}
    scratch |= {k: buf(B * V, D) for k in ("view", "dw")}
    for k in ("hin", "gin", "gout", "n1", "a1", "do1", "n2", "a2", "q2", "dq2", "do2"):
        scratch[k] = buf(B * T, D)
    scratch |= {k: buf(B * T, D, dtype=f32) for k in ("u1", "u2", "dn1", "dn2", "dm")}
    scratch |= {k: buf(B * T, 1, dtype=f32) for k in ("s1", "s2")}
    scratch |= {k: buf(B * T, 3 * D) for k in ("qkv1", "dqkv1")}
    scratch |= {k: buf(B * V, 2 * D) for k in ("kv2", "dkv2")}
    scratch["p1"] = buf(B, pairs, T, 2 * T, dtype=f32)
    W = max(H, 2 * V * pairs)
    scratch |= {"g": buf(B * T, H), "da": buf(B * T, W), "gp": buf(B * T, W, dtype=f32)}
    scratch |= {
        "w_sem": dma((8,)),
        "ex_sem": dma((8,)),
        "l_sem": dma((3,)),
        "gi_send": dma((B,)),
        "gi_recv": dma((B, S)),
        "gv_send": dma((B,)),
        "gv_recv": dma((B, S)),
        "f_send": dma((2 * B,)),
        "f_recv": dma((2 * B,)),
        "b_send": dma((2 * B,)),
        "b_recv": dma((2 * B,)),
        "si_send": dma((B, S)),
        "sv_send": dma((B, S)),
        "si_recv": dma((B,)),
        "sv_recv": dma((B,)),
        "r_send": dma((10, 8)),
        "r_recv": dma((10, 8)),
        "v_send": dma((3,)),
        "v_recv": dma((3,)),
    }
    names = list(args) + list(outs) + list(scratch)
    fused = lax.axis_size("dp") == 8
    *small, total = pl.pallas_call(
        partial(kernel, names, fused),
        out_shape=[pltpu.VMEM(s[:-1], s[-1]) for s in outs.values()],
        in_specs=[spec for _, spec in args.values()],
        out_specs=[vmem] * len(outs),
        scratch_shapes=list(scratch.values()),
        compiler_params=pltpu.CompilerParams(
            collective_id=0, has_side_effects=True, vmem_limit_bytes=50 << 20
        ),
        name="relay",
    )(*[value for value, _ in args.values()])
    if not fused:
        total, small[-1] = lax.psum((total, small[-1]), "dp")
    piece = D // 4
    wide, records, in_grad, view_grad, vector_grad = pl.pallas_call(
        widen,
        out_shape=[jax.ShapeDtypeStruct(mats.shape, f32)]
        + [jax.ShapeDtypeStruct(x.shape, x.dtype) for x in small],
        in_specs=[vmem] * 5,
        out_specs=[hbm] * 5,
        scratch_shapes=[pltpu.VMEM((4, piece, H), f32), dma((4,)), dma((4,))],
        compiler_params=pltpu.CompilerParams(vmem_limit_bytes=16 << 20),
        name="widen",
    )(total, *small)
    records = records.reshape(1, B, T, D)
    return records, in_grad, view_grad, wide, jnp.swapaxes(vector_grad, 0, 1)


def widen(total, *refs):
    small, wide, outs, slots, sems, small_sems = refs[:4], refs[4], refs[5:9], *refs[9:]
    held, piece, H = slots.shape
    D = total.shape[1]
    copies = [
        pltpu.make_async_copy(a, b, small_sems.at[i]) for i, (a, b) in enumerate(zip(small, outs))
    ]
    for copy in copies:
        copy.start()

    def write(i):
        t, rows = i * piece // D, pl.ds(i * piece % D, piece)
        return pltpu.make_async_copy(slots.at[i % held], wide.at[0, t, rows], sems.at[i % held])

    steps = 2 * D // piece
    for i in range(steps):
        if i >= held:
            write(i - held).wait()
        t, start = i * piece // D, i * piece % D
        for c in range(H // D):
            values = total[t * (H // D) + c, start : start + piece].astype(f32)
            slots[i % held, :, c * D : (c + 1) * D] = values
        write(i).start()
    for i in range(steps - held, steps):
        write(i).wait()
    for copy in copies:
        copy.wait()


def solution(mesh):
    in_specs = (
        P("dp", "section", None),
        P("dp", "section", None),
        P("section", None, None, None),
        P("section", None, None),
        P("dp"),
        P("dp"),
        P("dp", None),
        P("dp", None, None),
    )
    out_specs = (
        P("section", "dp", None, None),
        P("dp", "section", None),
        P("dp", "section", None),
        P("section", None, None, None),
        P("section", None, None),
    )
    return jax.shard_map(
        on_device, mesh=mesh, in_specs=in_specs, out_specs=out_specs, check_vma=False
    )
```

time: 187 us -> 163 us (0.87)
  Pallas kernels: 181 us -> 162 us
  local copies, waits for them, and re-layouts: 4.79 us -> 0 us
    pallas_call x1, Pallas kernels: 174 us -> 155 us  [on_device(): pl.pallas_call(partial(kernel, names, fused), out_shape=[pltpu.VMEM(s[:-1...]
    unnamed x11 -> x0, local copies, waits for them, and re-layouts: 4.05 us -> none
where the time goes in v3:
time: 163 us; the launch traced here: 162 us
  Pallas kernels  162 us (99%)
    pallas_call x1, Pallas kernels, on_device(): pl.pallas_call(partial(kernel, names, fused), out_shape=[pltpu.VMEM(s[:-1...  155 us
    pallas_call x1, Pallas kernels, on_device(): pl.pallas_call(widen, out_shape=[jax.ShapeDtypeStruct(mats.shape, f32)] +...  6.82 us

profile of v3, /device:TPU:9, one launch (start us, length us, event | category | flops | bytes accessed | tf_op | source)
XLA Modules:
  0.0 162.4 jit_solution(3091894402376441431)
XLA Ops:
  0.6 154.8 %relay.1 = (bf16[256,768]{1,0:T(8,128)(2,1)S(1)}, bf16[2,32,768]{2,1,0:T(8,128)(2,1)S(1)}, bf16[2,64,768]{2,1,0:T(8,128)(2,1)S(1)}, f32[7,1,768]{2,1,0:T(1,128)S(1)}, bf16[8,768,768]{2,1,0:T(8,128)(2,1)S(1)}) custom-call(bf16[2,32,768]{2,1,0:T(8,128)(2,1)} %refs_0_.1, bf16[2,64,768]{2,1,0:T(8,128)(2,1)} %refs_1_.1, bf16[1,2,768,3072]{3,2,1,0:T(8,128)(2,1)} %refs_2_.1, ...), custom_call_target="tpu_custom_call" | custom-call | tf_op jit(solution)/shard_map/relay/pallas_call | solution.py:931
  155.4 6.8 %widen.1 = (f32[1,2,768,3072]{3,2,1,0:T(8,128)}, bf16[256,768]{1,0:T(8,128)(2,1)}, bf16[2,32,768]{2,1,0:T(8,128)(2,1)}, bf16[2,64,768]{2,1,0:T(8,128)(2,1)}, f32[7,1,768]{2,1,0:T(1,128)}) custom-call(bf16[8,768,768]{2,1,0:T(8,128)(2,1)S(1)} %get-tuple-element.15.total, bf16[256,768]{1,0:T(8,128)(2,1)S(1)} %get-tuple-element.16.refs_0_, ...), custom_call_target="tpu_custom_call" | custom-call | tf_op jit(solution)/shard_map/widen/pallas_call | solution.py:945

commit v4 on v3

--- a/solution.py
+++ b/solution.py
@@ -53,34 +53,41 @@
     return jnp.concatenate([jnp.where(low, x, zero), jnp.where(low, zero, x)], axis=0)
 
 
-def softmax(scores, allowed):
-    scores = jnp.where(allowed, scores, -1000000000.0)
-    weights = jnp.exp(scores - jnp.max(scores, axis=-1, keepdims=True))
-    return weights * (1.0 / jnp.sum(weights, axis=-1, keepdims=True))
-
-
-def attend_pair(q, k, v, allowed):
-    n = k.shape[0]
-    scores = dot_t(q, halves(k))
-    weights = jnp.concatenate(
-        [softmax(scores[:, :n], allowed), softmax(scores[:, n:], allowed)], axis=1
-    )
-    return dot(weights.astype(bf16), halves(v)), weights
-
-
-def score_grads(v, weights, grad):
-    n = v.shape[0]
-    grad_weights = dot_t(grad, halves(v))
-    product = weights * grad_weights
-    parts = []
-    for part in (slice(0, n), slice(n, 2 * n)):
-        total = jnp.sum(product[:, part], axis=-1, keepdims=True)
-        parts.append((product[:, part] - weights[:, part] * total).astype(bf16))
-    return jnp.concatenate(parts, axis=1)
-
-
-def query_grads(k, grad_scores):
-    return dot(grad_scores, halves(k)) * (HEAD**-0.5)
+def attend(queries, keys, values, allowed):
+    n = keys[0].shape[0]
+    scores = [dot_t(q, halves(k)) for q, k in zip(queries, keys)]
+    split = [[jnp.where(allowed, x[:, h : h + n], -1000000000.0) for h in (0, n)] for x in scores]
+    peaks = [[jnp.max(x, axis=-1, keepdims=True) for x in pair] for pair in split]
+    raised = [[jnp.exp(x - m) for x, m in zip(*both)] for both in zip(split, peaks)]
+    shares = [[1.0 / jnp.sum(x, axis=-1, keepdims=True) for x in pair] for pair in raised]
+    weights = [
+        jnp.concatenate([x * m for x, m in zip(*both)], axis=1) for both in zip(raised, shares)
+    ]
+    outs = [dot(x.astype(bf16), halves(v)) for x, v in zip(weights, values)]
+    return outs, weights
+
+
+def score_grads(values, weights, grads):
+    n = values[0].shape[0]
+    grad_weights = [dot_t(x, halves(v)) for x, v in zip(grads, values)]
+    products = [x * y for x, y in zip(weights, grad_weights)]
+    totals = [
+        [jnp.sum(x[:, h : h + n], axis=-1, keepdims=True) for h in (0, n)] for x in products
+    ]
+    return [
+        jnp.concatenate(
+            [
+                (x[:, h : h + n] - y[:, h : h + n] * total).astype(bf16)
+                for h, total in zip((0, n), pair)
+            ],
+            axis=1,
+        )
+        for x, y, pair in zip(products, weights, totals)
+    ]
+
+
+def query_grads(keys, grad_scores):
+    return [dot(x, halves(k)) * (HEAD**-0.5) for x, k in zip(grad_scores, keys)]
 
 
 def stacked(x):
@@ -88,9 +95,9 @@
     return jnp.concatenate([x[:, :n], x[:, n:]], axis=0)
 
 
-def key_grads(q, weights, grad, grad_scores):
-    grad_k = t_dot(stacked(grad_scores), halves(q))
-    grad_v = t_dot(stacked(weights.astype(bf16)), halves(grad))
+def key_grads(queries, weights, grads, grad_scores):
+    grad_k = [t_dot(stacked(x), halves(q)) for x, q in zip(grad_scores, queries)]
+    grad_v = [t_dot(stacked(x.astype(bf16)), halves(y)) for x, y in zip(weights, grads)]
     return grad_k, grad_v
 
 
@@ -322,26 +329,32 @@
         gv[gain : gain + 1] = column_sum(grad[...] * unit[...])
         gv[shift : shift + 1] = column_sum(grad[...])
 
-    def key_columns(p, start):
-        return slice(start + p * PAIR, start + (p + 1) * PAIR)
+    def heads(ref, rows, start=0):
+        return [ref[rows, start + p * PAIR : start + (p + 1) * PAIR] for p in range(pairs)]
+
+    def put(ref, rows, values, start=0):
+        width = values[0].shape[1]
+        for p, value in enumerate(values):
+            ref[rows, start + p * width : start + (p + 1) * width] = value.astype(ref.dtype)
 
     def self_attend(r, rows, qkv, weights, attended):
         allowed = seg_q[r] == segments[pl.ds(r, 1)].astype(f32)
-        for p in range(pairs):
-            c, k, v = (key_columns(p, start) for start in (0, D, 2 * D))
-            out, kept = attend_pair(qkv[rows, c], qkv[rows, k], qkv[rows, v], allowed)
-            attended[rows, c] = out.astype(bf16)
-            weights[r, p] = kept
+        q, k, v = (heads(qkv, rows, start) for start in (0, D, 2 * D))
+        out, kept = attend(q, k, v, allowed)
+        put(attended, rows, out)
+        put(weights, rows, kept)
+
+    def held(weights, rows, n):
+        return [weights[rows, cols(p, 2 * n)] for p in range(pairs)]
 
     def self_attend_back(r, rows, qkv, weights, grad, dqkv):
-        for p in range(pairs):
-            c, k, v = (key_columns(p, start) for start in (0, D, 2 * D))
-            kept, do = weights[r, p], grad[rows, c]
-            ds = score_grads(qkv[rows, v], kept, do)
-            dqkv[rows, c] = query_grads(qkv[rows, k], ds).astype(bf16)
-            dk, dv = key_grads(qkv[rows, c], kept, do, ds)
-            dqkv[rows, k] = dk.astype(bf16)
-            dqkv[rows, v] = dv.astype(bf16)
+        q, k, v = (heads(qkv, rows, start) for start in (0, D, 2 * D))
+        kept, do = held(weights, rows, T), heads(grad, rows)
+        ds = score_grads(v, kept, do)
+        dk, dv = key_grads(q, kept, do, ds)
+        put(dqkv, rows, query_grads(k, ds))
+        put(dqkv, rows, dk, D)
+        put(dqkv, rows, dv, 2 * D)
 
     half = D // 2
 
@@ -361,44 +374,109 @@
         if fused:
             sum_core(b)
 
-    part_i, part_v = R["part_i"], R["part_v"]
-
-    def part_copy_i(r, k):
+    part_v = R["part_v"]
+
+    VH = 2 * VS
+
+    def part_copy(r, k):
         return remote(
-            gout.at[pl.ds(pl.multiple_of(r * T + k * TS, TS), TS)],
-            part_i.at[r],
-            R["si_send"].at[r, k],
-            R["si_recv"].at[r],
-            {"section": k},
-        )
-
-    def part_copy_v(r, k):
-        return remote(
-            R["dw"].at[pl.ds(pl.multiple_of(r * V + k * VS, VS), VS)],
+            R["dw"].at[pl.ds(pl.multiple_of(r * V + k * VH, VH), VH)],
             part_v.at[r],
             R["sv_send"].at[r, k],
             R["sv_recv"].at[r],
+            {"section": 3 * k},
+        )
+
+    def scatter_v(r):
+        for k in range(2):
+            part_copy(r, k).start()
+
+    def hand_i(r, k):
+        return remote(
+            R["fin_i"].at[pl.ds(r * T + k * TS, TS)],
+            in_grad.at[r],
+            R["hi_send"].at[r, k],
+            R["hi_recv"].at[r],
             {"section": k},
         )
 
-    def scatter_i(r):
-        for k in range(1, S):
-            part_copy_i(r, k).start()
-
-    def scatter_v(r):
-        for k in (0, 1, 3):
-            part_copy_v(r, k).start()
+    def hand_v(r, k):
+        return remote(
+            R["fin_v"].at[r, pl.ds((1 - k) * VS, VS)],
+            view_grad.at[r],
+            R["hv_send"].at[r, k],
+            R["hv_recv"].at[r],
+            {"section": 1 + k},
+        )
+
+    owed_i, owed_v = R["owed_i"], R["owed_v"]
+
+    def owed_i_copy(r):
+        rows = pl.ds(r * T, T)
+        return remote(
+            owed_i.at[rows], R["arr_i"].at[rows], R["oi_send"].at[r], R["oi_recv"].at[r], far
+        )
+
+    def owed_v_copy(r):
+        return remote(
+            owed_v.at[r], R["arr_v"].at[r], R["ov_send"].at[r], R["ov_recv"].at[r], far
+        )
+
+    def owed(t, rows):
+        return sum(
+            pick[r][t] * (1.0 - mix[r]) * rows[r].astype(f32) for r in range(B)
+        ).astype(bf16)
+
+    def combined(r, own, arrived):
+        return (mix[r] * own.astype(f32) + arrived.astype(f32)).astype(bf16)
+
+    def mixup_i():
+        rows = [gout[r * T : (r + 1) * T] for r in range(B)]
+        for t in range(B):
+            owed_i[t * T : (t + 1) * T] = owed(t, rows)
 
     rx, ry, rx2, ry2, core_in = (R[k] for k in ("rx", "ry", "rx2", "ry2", "core_in"))
     quarter, eighth = half // 4, half // 8
     own = core * half
     a0, b0 = own, own + half // 2
     a_own, a_far = a0 + x_bit * quarter, a0 + (1 - x_bit) * quarter
-    b_own, b_far = b0 + y_bit * quarter, b0 + (1 - y_bit) * quarter
     a_end, a_out = a_own + y_bit * eighth, a_own + (1 - y_bit) * eighth
-    b_end, b_out = b_own + x_bit * eighth, b_own + (1 - x_bit) * eighth
-    blocks = jnp.where(z == 0, 4, 8)
-    shift = jnp.where(z == 2, 4, 0)
+
+    def turned_round(b):
+        return jnp.where(b < jnp.where(z == 0, 2, jnp.where(z == 3, 1, 0)), 1, 0)
+
+    def second_half(b):
+        flip = turned_round(b)
+        first = y_bit + flip * (x_bit - y_bit)
+        then = x_bit + flip * (y_bit - x_bit)
+        mine, other = b0 + first * quarter, b0 + (1 - first) * quarter
+        return mine, other, mine + then * eighth, mine + (1 - then) * eighth
+
+    def first_way(b):
+        flip = turned_round(b)
+        return {"dp": (1 - flip) * far["dp"] + flip * x_next["dp"]}
+
+    def second_way(b):
+        flip = turned_round(b)
+        return {"dp": flip * far["dp"] + (1 - flip) * x_next["dp"]}
+    LENT, TAKEN = 0, 4
+    own_blocks = jnp.where(z == 0, 4, 8)
+    blocks = jnp.where(z == 0, 5, jnp.where(z == 1, 7, 8))
+    wrap = jnp.where(z == 0, 5, 8)
+    shift = jnp.where(z == 2, 4, jnp.where(z == 1, 1, 0))
+    shift_back = jnp.where(z == 0, TAKEN, shift)
+
+    def lend():
+        rows = part(own, half)
+        return remote(
+            G.at[LENT, rows], G.at[TAKEN, rows], R["lend_send"], R["lend_recv"], {"section": 0}
+        )
+
+    def give_back():
+        rows = part(own, half)
+        return remote(
+            w.at[TAKEN, rows], w.at[LENT, rows], R["back_send"], R["back_recv"], {"section": 1}
+        )
 
     def part(start, length):
         return pl.ds(pl.multiple_of(start, eighth), length)
@@ -410,25 +488,29 @@
         return remote(G.at[b, part(a_far, quarter)], rx.at[b], *sems(1, b), x_next)
 
     def scatter_y(b):
-        return remote(G.at[b, part(b_far, quarter)], ry.at[b], *sems(2, b), far)
+        rows = part(second_half(b)[1], quarter)
+        return remote(G.at[b, rows], ry.at[b], *sems(2, b), first_way(b))
 
     def scatter_xy(b):
         return remote(G.at[b, part(a_out, eighth)], ry2.at[b], *sems(3, b), far)
 
     def scatter_yx(b):
-        return remote(G.at[b, part(b_out, eighth)], rx2.at[b], *sems(4, b), x_next)
+        rows = part(second_half(b)[3], eighth)
+        return remote(G.at[b, rows], rx2.at[b], *sems(4, b), second_way(b))
 
     def spread_y(b):
         return remote(final(b, a_end, eighth), final(b, a_end, eighth), *sems(5, b), far)
 
     def spread_x(b):
-        return remote(final(b, b_end, eighth), final(b, b_end, eighth), *sems(6, b), x_next)
+        rows = final(b, second_half(b)[2], eighth)
+        return remote(rows, rows, *sems(6, b), second_way(b))
 
     def spread_yx(b):
         return remote(final(b, a_own, quarter), final(b, a_own, quarter), *sems(7, b), x_next)
 
     def spread_xy(b):
-        return remote(final(b, b_own, quarter), final(b, b_own, quarter), *sems(8, b), far)
+        rows = final(b, second_half(b)[0], quarter)
+        return remote(rows, rows, *sems(8, b), first_way(b))
 
     def spread_core(b):
         return remote(final(b, own, half), final(b, own, half), *sems(9, b), beside)
@@ -445,8 +527,21 @@
     def sum_core(b):
         core_send(b).wait_recv()
         add(b, own, half, core_in)
-        scatter_x(b).start()
-        scatter_y(b).start()
+        lent = (z == 1) & (b == LENT)
+
+        @pl.when(lent)
+        def _():
+            lend().start()
+
+        @pl.when(jnp.logical_not(lent))
+        def _():
+            scatter_x(b).start()
+            scatter_y(b).start()
+
+    def take():
+        lend().wait_recv()
+        scatter_x(TAKEN).start()
+        scatter_y(TAKEN).start()
 
     n1, u1, s1, p1, a1 = R["n1"], R["u1"], R["s1"], R["p1"], R["a1"]
     qkv1, dqkv1, do1, dn1 = R["qkv1"], R["dqkv1"], R["do1"], R["dn1"]
@@ -455,7 +550,6 @@
     view, dm = R["view"], R["dm"]
     g, gp, da = R["g"], R["gp"], R["da"]
     p2, ds2 = gp, da
-    wide_pair = 2 * V
     SCALE = HEAD**-0.5
 
     def wide_t(first, count):
@@ -492,23 +586,25 @@
             dn = dot(dqkv1[rows], wide_t(0, 3))
             dn1[rows] = dn
             gout[rows] = (e.astype(f32) + norm_out(dn, rows, u1, s1, 0)).astype(bf16)
-            scatter_i(r)
 
         each_row(backward)
         for b in range(3):
             produce(b, t_dot(n1[...], dqkv1[:, cols(b)]))
+        mixup_i()
         follow(0)
+        owed_i_copy(0).start()
         produce(3, t_dot(a1[...], gin[...]))
-        for b in range(1, 4):
+        follow(1)
+        for r in range(1, B):
+            owed_i_copy(r).start()
+        for b in range(2, 4):
             follow(b)
         norm_sums(dn1, u1, 0, 1)
         gv[2:3] = column_sum(dqkv1[:, cols(2)])
         gv[4:5] = column_sum(gin[...])
         gv[5:6] = column_sum(dqkv1[:, cols(0)])
-        for r in range(B):
-            part_i[r] = gout[r * T : r * T + TS]
         if fused:
-            for b in range(4, 8):
+            for b in range(5, 8):
                 w[b] = jnp.zeros((D, D), bf16)
         else:
             for b in range(4, 8):
@@ -642,12 +738,10 @@
             h = hin[rows].astype(f32)
             n = norm_in(h, rows, u2, s2, n2, 0, 1)
             q2[rows] = dot(n, w[0]).astype(bf16) * SCALE
-            allowed = seg_q[r] == seg_v[r]
-            for p in range(pairs):
-                c, v = (key_columns(p, start) for start in (0, D))
-                out, kept = attend_pair(q2[rows, c], kv2[wide, c], kv2[wide, v], allowed)
-                a2[rows, c] = out.astype(bf16)
-                p2[rows, cols(p, wide_pair)] = kept
+            keys, values = heads(kv2, wide), heads(kv2, wide, D)
+            out, kept = attend(heads(q2, rows), keys, values, seg_q[r] == seg_v[r])
+            put(a2, rows, out)
+            put(p2, rows, kept)
             m = h + dot(a2[rows], w[3]) + vec[4]
             n = norm_in(m, rows, u1, s1, n1, 2, 3)
             q = (dot(n, w[4]) + vec[5]).astype(bf16)
@@ -672,11 +766,9 @@
             dmid = e.astype(f32) + norm_out(dn, rows, u1, s1, 2)
             dm[rows] = dmid
             do2[rows] = dot(dmid.astype(bf16), wt[3]).astype(bf16)
-            for p in range(pairs):
-                c, v = (key_columns(p, start) for start in (0, D))
-                ds = score_grads(kv2[wide, v], p2[rows, cols(p, wide_pair)], do2[rows, c])
-                ds2[rows, cols(p, wide_pair)] = ds
-                dq2[rows, c] = query_grads(kv2[wide, c], ds).astype(bf16)
+            ds = score_grads(heads(kv2, wide, D), held(p2, rows, V), heads(do2, rows))
+            put(ds2, rows, ds)
+            put(dq2, rows, query_grads(heads(kv2, wide), ds))
             dn = dot(dq2[rows], wt[0])
             dn2[rows] = dn
             gout[rows] = (dmid + norm_out(dn, rows, u2, s2, 0)).astype(bf16)
@@ -691,15 +783,13 @@
 
         def source_grad(r):
             rows, wide = at(r, T), at(r, V)
-            for p in range(pairs):
-                c, v = (key_columns(p, start) for start in (0, D))
-                x = cols(p, wide_pair)
-                dk, dv = key_grads(q2[rows, c], p2[rows, x], do2[rows, c], ds2[rows, x])
-                dkv2[wide, c] = dk.astype(bf16)
-                dkv2[wide, v] = dv.astype(bf16)
+            dk, dv = key_grads(
+                heads(q2, rows), held(p2, rows, V), heads(do2, rows), held(ds2, rows, V)
+            )
+            put(dkv2, wide, dk)
+            put(dkv2, wide, dv, D)
             dw = dot_t(dkv2[wide, cols(0)], w[1]) + dot_t(dkv2[wide, cols(1)], w[2])
             R["dw"][wide] = dw.astype(bf16)
-            scatter_v(r)
 
         each_row(source_grad)
         for b in range(2):
@@ -712,51 +802,66 @@
             follow(b)
         norm_sums(dn1, u1, 2, 3)
         norm_sums(dn2, u2, 0, 1)
+        each_row(scatter_v)
         gv[4:5] = column_sum(dm[...])
         gv[5:6] = column_sum(dqkv1[:, cols(0)])
         gv[6:7] = column_sum(gin[...])
+
+    def mixup_v():
         for r in range(B):
-            part_v[r] = R["dw"][r * V + 2 * VS : r * V + 3 * VS]
-
-    owed_i, owed_v = R["owed_i"], R["owed_v"]
-    owed_to = [
-        remote(owed_i, R["arr_i"], ex.at[4], ex.at[5], far),
-        remote(owed_v, R["arr_v"], ex.at[6], ex.at[7], far),
-    ]
-
-    def mixup_back():
-        @pl.when(z != 0)
-        def _():
-            for r in range(B):
-                part_copy_i(r, 0).wait_recv()
-
-        @pl.when(z != 2)
-        def _():
-            for r in range(B):
-                part_copy_v(r, 0).wait_recv()
-
-        for part, owed, copy in zip((part_i, part_v), (owed_i, owed_v), owed_to):
-            for t in range(B):
-                owed[t] = sum(
-                    pick[r][t] * (1.0 - mix[r]) * part[r].astype(f32) for r in range(B)
-                ).astype(bf16)
-            copy.start()
-
-    def mixup_end():
-        for part, arrived, out, copy in zip(
-            (part_i, part_v), (R["arr_i"], R["arr_v"]), (in_grad, view_grad), owed_to
-        ):
-            copy.wait_recv()
-            for r in range(B):
-                out[r] = (mix[r] * part[r].astype(f32) + arrived[r].astype(f32)).astype(bf16)
-            copy.wait_send()
+            part_copy(r, 0).wait_recv()
+        rows = [part_v[r] for r in range(B)]
+        for t in range(B):
+            owed_v[t] = owed(t, rows)
+
+    def mixup_i_end():
+        for r in range(B):
+            owed_i_copy(r).wait()
+        for r in range(B):
+            rows = slice(r * T, (r + 1) * T)
+            R["fin_i"][rows] = combined(r, gout[rows], R["arr_i"][rows])
+        for r in range(B):
+            for k in range(1, S):
+                hand_i(r, k).start()
+            in_grad[r] = R["fin_i"][r * T : r * T + TS]
+
+    def mixup_v_end(k):
+        for r in range(B):
+            owed_v_copy(r).wait()
+        for r in range(B):
+            R["fin_v"][r] = combined(r, part_v[r], R["arr_v"][r])
+        for r in range(B):
+            hand_v(r, k).start()
+            view_grad[r] = R["fin_v"][r, k * VS : (k + 1) * VS]
+
+    def mixup_handed():
+        for r in range(B):
+
+            @pl.when(z != 0)
+            def _():
+                hand_i(r, 1).wait_recv()
+
+            @pl.when((z == 1) | (z == 2))
+            def _():
+                hand_v(r, 0).wait_recv()
+
+            @pl.when(z == 0)
+            def _():
+                for k in range(1, S):
+                    hand_i(r, k).wait_send()
+
+            for end, k in ((0, 0), (3, 1)):
+
+                @pl.when(z == end)
+                def _():
+                    hand_v(r, k).wait_send()
 
     def sum_first(b):
         scatter_x(b).wait_recv()
         add(b, a_own, quarter, rx)
         scatter_xy(b).start()
         scatter_y(b).wait_recv()
-        add(b, b_own, quarter, ry)
+        add(b, second_half(b)[0], quarter, ry)
         scatter_yx(b).start()
 
     def sum_second(b):
@@ -764,8 +869,12 @@
         finish(b, a_end, ry2)
         spread_y(b).start()
         scatter_yx(b).wait_recv()
-        finish(b, b_end, rx2)
+        finish(b, second_half(b)[2], rx2)
         spread_x(b).start()
+
+        @pl.when((z == 3) & (b < B))
+        def _():
+            owed_v_copy(b).start()
 
     def pass_on(b):
         spread_y(b).wait_recv()
@@ -773,19 +882,35 @@
         spread_x(b).wait_recv()
         spread_xy(b).start()
 
+        @pl.when((z == 0) & (b < B))
+        def _():
+            owed_v_copy(b).start()
+
     def pass_core(b):
         spread_yx(b).wait_recv()
         spread_xy(b).wait_recv()
-        spread_core(b).start()
+        taken = (z == 0) & (b == TAKEN)
+
+        @pl.when(taken)
+        def _():
+            give_back().start()
+
+        @pl.when(jnp.logical_not(taken))
+        def _():
+            spread_core(b).start()
 
     def arrive(b):
         spread_core(b).wait_recv()
 
     def sent(b):
-        for copy in (core_send, scatter_x, scatter_y, scatter_xy, scatter_yx, spread_y):
+        for copy in (scatter_x, scatter_y, scatter_xy, scatter_yx, spread_y, spread_x):
             copy(b).wait_send()
-        for copy in (spread_x, spread_yx, spread_xy, spread_core):
+        for copy in (spread_yx, spread_xy):
             copy(b).wait_send()
+
+    def core_sent(b):
+        core_send(b).wait_send()
+        spread_core(b).wait_send()
 
     def vector_round(k, device):
         return remote(gv, R["gv_in"].at[k], R["v_send"].at[k], R["v_recv"].at[k], device)
@@ -795,44 +920,97 @@
         copy.wait()
         gv[...] += R["gv_in"][k]
 
+    def loop(first, last, step):
+        lax.fori_loop(first, last, lambda i, c: (step(i), c)[1], 0)
+
     def each_block(step):
-        lax.fori_loop(0, blocks, lambda i, c: (step(lax.rem(i + shift, 8)), c)[1], 0)
+        loop(0, blocks, lambda i: step(lax.rem(i + shift, wrap)))
+
+    def each_back(step):
+        loop(0, blocks, lambda i: step(lax.rem(i + shift_back, wrap)))
 
     if fused:
         vector_round(0, beside).start()
         vector_sum(0, beside)
         vector_round(1, x_next).start()
+
+        @pl.when(z == 0)
+        def _():
+            take()
+
         each_block(sum_first)
         vector_sum(1, x_next)
         vector_round(2, far).start()
-        each_block(sum_second)
+
+        @pl.when(z == 3)
+        def _():
+            mixup_v()
+
+        each_back(sum_second)
         vector_sum(2, far)
-        mixup_back()
-        each_block(pass_on)
-        each_block(pass_core)
-        each_block(arrive)
-        mixup_end()
+
+        @pl.when(z == 0)
+        def _():
+            mixup_i_end()
+            mixup_v()
+
+        each_back(pass_on)
+
+        @pl.when(z == 3)
+        def _():
+            mixup_v_end(1)
+
+        each_back(pass_core)
+
+        @pl.when(z == 0)
+        def _():
+            mixup_v_end(0)
+
+
+        @pl.when(z == 1)
+        def _():
+            give_back().wait_recv()
+            spread_core(LENT).start()
+
+        loop(0, own_blocks, arrive)
+        mixup_handed()
         each_block(sent)
+        loop(0, own_blocks, core_sent)
+
+        @pl.when(z == 1)
+        def _():
+            lend().wait_send()
+
+        @pl.when(z == 0)
+        def _():
+            give_back().wait_send()
+            w[TAKEN] = jnp.zeros((D, D), bf16)
+
     else:
-        mixup_back()
-        mixup_end()
+        @pl.when(z == 0)
+        def _():
+            mixup_i_end()
+
+        @pl.when((z == 0) | (z == 3))
+        def _():
+            mixup_v()
+            for r in range(B):
+                owed_v_copy(r).start()
+
+        for end, k in ((0, 0), (3, 1)):
+            pl.when(z == end)(partial(mixup_v_end, k))
+        mixup_handed()
         for b in range(8):
             w[b] = G[b]
 
     for i in range(vec.shape[0]):
         R["gv_out"][i] = gv[i : i + 1]
-
-    @pl.when(z == 0)
-    def _():
-        for r in range(B):
-            for k in range(1, S):
-                part_copy_i(r, k).wait_send()
 
     @pl.when(z == 2)
     def _():
         for r in range(B):
-            for k in (0, 1, 3):
-                part_copy_v(r, k).wait_send()
+            for k in range(2):
+                part_copy(r, k).wait_send()
 
     for r in range(B):
 
@@ -893,8 +1071,11 @@
     scratch |= {k: buf(8, D // 16, D) for k in ("rx2", "ry2")}
     scratch |= {"gv": buf(8, D, dtype=f32), "gv_in": buf(3, 8, D, dtype=f32)}
     scratch |= {"seg_q": buf(B, T, 1, dtype=f32), "seg_v": buf(B, 1, V, dtype=f32)}
-    for k in ("own", "far", "stage", "part", "owed", "arr"):
+    for k in ("own", "far", "stage"):
         scratch |= {k + "_i": buf(B, TS, D), k + "_v": buf(B, VS, D)}
+    for k in ("owed", "arr", "fin"):
+        scratch |= {k + "_i": buf(B * T, D), k + "_v": buf(B, 2 * VS, D)}
+    scratch["part_v"] = buf(B, 2 * VS, D)
     scratch |= {k: buf(B * V, D) for k in ("view", "dw")}
     for k in ("hin", "gin", "gout", "n1", "a1", "do1", "n2", "a2", "q2", "dq2", "do2"):
         scratch[k] = buf(B * T, D)
@@ -902,12 +1083,16 @@
     scratch |= {k: buf(B * T, 1, dtype=f32) for k in ("s1", "s2")}
     scratch |= {k: buf(B * T, 3 * D) for k in ("qkv1", "dqkv1")}
     scratch |= {k: buf(B * V, 2 * D) for k in ("kv2", "dkv2")}
-    scratch["p1"] = buf(B, pairs, T, 2 * T, dtype=f32)
+    scratch["p1"] = buf(B * T, 2 * T * pairs, dtype=f32)
     W = max(H, 2 * V * pairs)
     scratch |= {"g": buf(B * T, H), "da": buf(B * T, W), "gp": buf(B * T, W, dtype=f32)}
     scratch |= {
         "w_sem": dma((8,)),
-        "ex_sem": dma((8,)),
+        "ex_sem": dma((4,)),
+        "oi_send": dma((B,)),
+        "oi_recv": dma((B,)),
+        "ov_send": dma((B,)),
+        "ov_recv": dma((B,)),
         "l_sem": dma((3,)),
         "gi_send": dma((B,)),
         "gi_recv": dma((B, S)),
@@ -917,10 +1102,16 @@
         "f_recv": dma((2 * B,)),
         "b_send": dma((2 * B,)),
         "b_recv": dma((2 * B,)),
-        "si_send": dma((B, S)),
-        "sv_send": dma((B, S)),
-        "si_recv": dma((B,)),
+        "sv_send": dma((B, 2)),
         "sv_recv": dma((B,)),
+        "hi_send": dma((B, S)),
+        "hi_recv": dma((B,)),
+        "hv_send": dma((B, 2)),
+        "hv_recv": dma((B,)),
+        "lend_send": dma,
+        "lend_recv": dma,
+        "back_send": dma,
+        "back_recv": dma,
         "r_send": dma((10, 8)),
         "r_recv": dma((10, 8)),
         "v_send": dma((3,)),

time: 163 us -> 148 us (0.908); the launches traced: 162 us -> 146 us
  Pallas kernels: 162 us -> 145 us
    pallas_call x1, Pallas kernels: 155 us -> 138 us  [on_device(): pl.pallas_call(partial(kernel, names, fused), out_shape=[pltpu.VMEM(s[:-1...]
where the time goes in v4:
time: 148 us; the launch traced here: 146 us
  Pallas kernels  145 us (98%)
    pallas_call x1, Pallas kernels, on_device(): pl.pallas_call(partial(kernel, names, fused), out_shape=[pltpu.VMEM(s[:-1...  138 us
    pallas_call x1, Pallas kernels, on_device(): pl.pallas_call(widen, out_shape=[jax.ShapeDtypeStruct(mats.shape, f32)] +...  6.82 us

profile of v4, /device:TPU:9, one launch (start us, length us, event | category | flops | bytes accessed | tf_op | source)
XLA Modules:
  0.0 145.7 jit_solution(16560189271045767892)
XLA Ops:
  0.6 138.0 %relay.1 = (bf16[256,768]{1,0:T(8,128)(2,1)S(1)}, bf16[2,32,768]{2,1,0:T(8,128)(2,1)S(1)}, bf16[2,64,768]{2,1,0:T(8,128)(2,1)S(1)}, f32[7,1,768]{2,1,0:T(1,128)S(1)}, bf16[8,768,768]{2,1,0:T(8,128)(2,1)S(1)}) custom-call(bf16[2,32,768]{2,1,0:T(8,128)(2,1)} %refs_0_.1, bf16[2,64,768]{2,1,0:T(8,128)(2,1)} %refs_1_.1, bf16[1,2,768,3072]{3,2,1,0:T(8,128)(2,1)} %refs_2_.1, ...), custom_call_target="tpu_custom_call" | custom-call | tf_op jit(solution)/shard_map/relay/pallas_call | solution.py:1122
  138.7 6.8 %widen.1 = (f32[1,2,768,3072]{3,2,1,0:T(8,128)}, bf16[256,768]{1,0:T(8,128)(2,1)}, bf16[2,32,768]{2,1,0:T(8,128)(2,1)}, bf16[2,64,768]{2,1,0:T(8,128)(2,1)}, f32[7,1,768]{2,1,0:T(1,128)}) custom-call(bf16[8,768,768]{2,1,0:T(8,128)(2,1)S(1)} %get-tuple-element.15.total, bf16[256,768]{1,0:T(8,128)(2,1)S(1)} %get-tuple-element.16.refs_0_, ...), custom_call_target="tpu_custom_call" | custom-call | tf_op jit(solution)/shard_map/widen/pallas_call | solution.py:1136

commit v5 on v4

--- a/solution.py
+++ b/solution.py
@@ -165,12 +165,6 @@
         pl.semaphore_signal(barrier, inc=1, device_id=other, device_id_type=MESH)
     own_i.start()
     own_v.start()
-    for b in range(8):
-        table(b).start()
-
-    @pl.when(z == S - 1)
-    def _():
-        own_cot.start()
 
     gv[...] = jnp.zeros_like(gv)
     pick = [[(partner[r] == j).astype(f32) for j in range(B)] for r in range(B)]
@@ -233,6 +227,13 @@
             R["stage_i"][r] = mixed
             gather_i(r, z).start()
 
+    for b in range(8):
+        table(b).start()
+
+    @pl.when(z == S - 1)
+    def _():
+        own_cot.start()
+
     @pl.when(z != 0)
     def _():
         far_v.start()
@@ -512,8 +513,9 @@
         rows = final(b, second_half(b)[0], quarter)
         return remote(rows, rows, *sems(8, b), first_way(b))
 
-    def spread_core(b):
-        return remote(final(b, own, half), final(b, own, half), *sems(9, b), beside)
+    def spread_core(b, k):
+        rows = final(b, own + k * (half // 2), half // 2)
+        return remote(rows, rows, *sems(9 + k, b), beside)
 
     def add(b, start, length, arrived):
         rows = part(start, length)
@@ -610,10 +612,6 @@
             for b in range(4, 8):
                 G[b] = jnp.zeros((D, D), bf16)
 
-    def feed_hidden(n, c):
-        a = dot(n, w[c]) + vec[2 + c]
-        return gelu_parts(a)
-
     def feed_grads(first, last, left, right, start):
         def one(c, _):
             produce(first + c, t_dot(left[...], right[:, at(c, D)]))
@@ -638,15 +636,15 @@
             entered(i)
             h = hin[rows].astype(f32)
             n = norm_in(h, rows, u1, s1, n1, 0, 1)
-            out = h + vec[6]
-            for c in range(4):
-                active, slope = feed_hidden(n, c)
-                active = active.astype(bf16)
-                g[rows, cols(c)] = active
-                gp[rows, cols(c)] = slope
-                out += dot(active, wt[4 + c])
+            hidden = [dot(n, w[c]) + vec[2 + c] for c in range(4)]
+            parts = [gelu_parts(a) for a in hidden]
+            actives = [active.astype(bf16) for active, _ in parts]
+            out = sum([dot(active, wt[4 + c]) for c, active in enumerate(actives)], h + vec[6])
             records[rows] = out.astype(bf16)
             forward_hop(i).start()
+            for c in range(4):
+                g[rows, cols(c)] = actives[c]
+                gp[rows, cols(c)] = parts[c][1]
 
         each_chunk(forward)
 
@@ -654,12 +652,11 @@
             rows = at(i, CH)
             returned(i)
             e = gin[rows]
-            dn = jnp.zeros((CH, D), f32)
+            dgs = [dot(e, w[4 + c]) for c in range(4)]
+            dcs = [(dg * gp[rows, cols(c)]).astype(bf16) for c, dg in enumerate(dgs)]
+            dn = sum([dot(dc, wt[c]) for c, dc in enumerate(dcs)])
             for c in range(4):
-                dg = dot(e, w[4 + c])
-                dc = (dg * gp[rows, cols(c)]).astype(bf16)
-                da[rows, cols(c)] = dc
-                dn += dot(dc, wt[c])
+                da[rows, cols(c)] = dcs[c]
             dn1[rows] = dn
             gout[rows] = (e.astype(f32) + norm_out(dn, rows, u1, s1, 0)).astype(bf16)
             backward_hop(i).start()
@@ -690,13 +687,13 @@
             entered(i)
             e = cot[rows]
             n = norm_in(hin[rows].astype(f32), rows, u1, s1, n1, 0, 1)
-            dn = jnp.zeros((CH, D), f32)
+            hidden = [dot(n, w[c]) + vec[2 + c] for c in range(4)]
+            parts = [gelu_parts(a) for a in hidden]
+            dcs = [(gp[rows, cols(c)] * parts[c][1]).astype(bf16) for c in range(4)]
+            dn = sum([dot(dc, wt[c]) for c, dc in enumerate(dcs)])
             for c in range(4):
-                active, slope = feed_hidden(n, c)
-                g[rows, cols(c)] = active.astype(bf16)
-                dc = (gp[rows, cols(c)] * slope).astype(bf16)
-                da[rows, cols(c)] = dc
-                dn += dot(dc, wt[c])
+                g[rows, cols(c)] = parts[c][0].astype(bf16)
+                da[rows, cols(c)] = dcs[c]
             dn1[rows] = dn
             gout[rows] = (e.astype(f32) + norm_out(dn, rows, u1, s1, 0)).astype(bf16)
             backward_hop(i).start()
@@ -887,9 +884,14 @@
             owed_v_copy(b).start()
 
     def pass_core(b):
+        taken = (z == 0) & (b == TAKEN)
         spread_yx(b).wait_recv()
+
+        @pl.when(jnp.logical_not(taken))
+        def _():
+            spread_core(b, 0).start()
+
         spread_xy(b).wait_recv()
-        taken = (z == 0) & (b == TAKEN)
 
         @pl.when(taken)
         def _():
@@ -897,10 +899,11 @@
 
         @pl.when(jnp.logical_not(taken))
         def _():
-            spread_core(b).start()
+            spread_core(b, 1).start()
 
     def arrive(b):
-        spread_core(b).wait_recv()
+        spread_core(b, 0).wait_recv()
+        spread_core(b, 1).wait_recv()
 
     def sent(b):
         for copy in (scatter_x, scatter_y, scatter_xy, scatter_yx, spread_y, spread_x):
@@ -910,7 +913,8 @@
 
     def core_sent(b):
         core_send(b).wait_send()
-        spread_core(b).wait_send()
+        spread_core(b, 0).wait_send()
+        spread_core(b, 1).wait_send()
 
     def vector_round(k, device):
         return remote(gv, R["gv_in"].at[k], R["v_send"].at[k], R["v_recv"].at[k], device)
@@ -960,17 +964,21 @@
         def _():
             mixup_v_end(1)
 
-        each_back(pass_core)
+        most = blocks - 2
+        loop(0, most, lambda i: pass_core(lax.rem(i + shift_back, wrap)))
 
         @pl.when(z == 0)
         def _():
             mixup_v_end(0)
 
+        loop(most, blocks, lambda i: pass_core(lax.rem(i + shift_back, wrap)))
+
 
         @pl.when(z == 1)
         def _():
             give_back().wait_recv()
-            spread_core(LENT).start()
+            spread_core(LENT, 0).start()
+            spread_core(LENT, 1).start()
 
         loop(0, own_blocks, arrive)
         mixup_handed()
@@ -1112,8 +1120,8 @@
         "lend_recv": dma,
         "back_send": dma,
         "back_recv": dma,
-        "r_send": dma((10, 8)),
-        "r_recv": dma((10, 8)),
+        "r_send": dma((11, 8)),
+        "r_recv": dma((11, 8)),
         "v_send": dma((3,)),
         "v_recv": dma((3,)),
     }

time: 148 us -> 145 us (0.980)
  Pallas kernels: 145 us -> 143 us
    pallas_call x1, Pallas kernels: 138 us -> 136 us  [on_device(): pl.pallas_call(partial(kernel, names, fused), out_shape=[pltpu.VMEM(s[:-1...]
where the time goes in v5:
time: 145 us; the launch traced here: 144 us
  Pallas kernels  143 us (99%)
    pallas_call x1, Pallas kernels, on_device(): pl.pallas_call(partial(kernel, names, fused), out_shape=[pltpu.VMEM(s[:-1...  136 us
    pallas_call x1, Pallas kernels, on_device(): pl.pallas_call(widen, out_shape=[jax.ShapeDtypeStruct(mats.shape, f32)] +...  6.82 us

profile of v5, /device:TPU:9, one launch (start us, length us, event | category | flops | bytes accessed | tf_op | source)
XLA Modules:
  0.0 143.6 jit_solution(7754728750092392598)
XLA Ops:
  0.6 136.0 %relay.1 = (bf16[256,768]{1,0:T(8,128)(2,1)S(1)}, bf16[2,32,768]{2,1,0:T(8,128)(2,1)S(1)}, bf16[2,64,768]{2,1,0:T(8,128)(2,1)S(1)}, f32[7,1,768]{2,1,0:T(1,128)S(1)}, bf16[8,768,768]{2,1,0:T(8,128)(2,1)S(1)}) custom-call(bf16[2,32,768]{2,1,0:T(8,128)(2,1)} %refs_0_.1, bf16[2,64,768]{2,1,0:T(8,128)(2,1)} %refs_1_.1, bf16[1,2,768,3072]{3,2,1,0:T(8,128)(2,1)} %refs_2_.1, ...), custom_call_target="tpu_custom_call" | custom-call | tf_op jit(solution)/shard_map/relay/pallas_call | solution.py:1130
  136.6 6.8 %widen.1 = (f32[1,2,768,3072]{3,2,1,0:T(8,128)}, bf16[256,768]{1,0:T(8,128)(2,1)}, bf16[2,32,768]{2,1,0:T(8,128)(2,1)}, bf16[2,64,768]{2,1,0:T(8,128)(2,1)}, f32[7,1,768]{2,1,0:T(1,128)}) custom-call(bf16[8,768,768]{2,1,0:T(8,128)(2,1)S(1)} %get-tuple-element.15.total, bf16[256,768]{1,0:T(8,128)(2,1)S(1)} %get-tuple-element.16.refs_0_, ...), custom_call_target="tpu_custom_call" | custom-call | tf_op jit(solution)/shard_map/widen/pallas_call | solution.py:1144

commit v6 on v5

--- a/solution.py
+++ b/solution.py
@@ -905,14 +905,15 @@
         spread_core(b, 0).wait_recv()
         spread_core(b, 1).wait_recv()
 
-    def sent(b):
+    def sent_early(b):
         for copy in (scatter_x, scatter_y, scatter_xy, scatter_yx, spread_y, spread_x):
             copy(b).wait_send()
-        for copy in (spread_yx, spread_xy):
-            copy(b).wait_send()
+
+    def sent(b):
+        spread_yx(b).wait_send()
+        spread_xy(b).wait_send()
 
     def core_sent(b):
-        core_send(b).wait_send()
         spread_core(b, 0).wait_send()
         spread_core(b, 1).wait_send()
 
@@ -924,6 +925,36 @@
         copy.wait()
         gv[...] += R["gv_in"][k]
 
+    def relay_sent():
+        for i in range(vec.shape[0]):
+            R["gv_out"][i] = gv[i : i + 1]
+
+        @pl.when(z == 2)
+        def _():
+            for r in range(B):
+                for k in range(2):
+                    part_copy(r, k).wait_send()
+
+        for r in range(B):
+
+            @pl.when(z != 0)
+            def _():
+                gather_i(r, z).wait_send()
+
+            @pl.when(z != 2)
+            def _():
+                gather_v(r, z).wait_send()
+
+        for i in range(chunks):
+
+            @pl.when(z != 0)
+            def _():
+                backward_hop(i).wait_send()
+
+            @pl.when(z != S - 1)
+            def _():
+                forward_hop(i).wait_send()
+
     def loop(first, last, step):
         lax.fori_loop(first, last, lambda i, c: (step(i), c)[1], 0)
 
@@ -959,6 +990,9 @@
             mixup_v()
 
         each_back(pass_on)
+        each_block(sent_early)
+        loop(0, own_blocks, lambda b: core_send(b).wait_send())
+        relay_sent()
 
         @pl.when(z == 3)
         def _():
@@ -1008,37 +1042,9 @@
         for end, k in ((0, 0), (3, 1)):
             pl.when(z == end)(partial(mixup_v_end, k))
         mixup_handed()
+        relay_sent()
         for b in range(8):
             w[b] = G[b]
-
-    for i in range(vec.shape[0]):
-        R["gv_out"][i] = gv[i : i + 1]
-
-    @pl.when(z == 2)
-    def _():
-        for r in range(B):
-            for k in range(2):
-                part_copy(r, k).wait_send()
-
-    for r in range(B):
-
-        @pl.when(z != 0)
-        def _():
-            gather_i(r, z).wait_send()
-
-        @pl.when(z != 2)
-        def _():
-            gather_v(r, z).wait_send()
-
-    for i in range(chunks):
-
-        @pl.when(z != 0)
-        def _():
-            backward_hop(i).wait_send()
-
-        @pl.when(z != S - 1)
-        def _():
-            forward_hop(i).wait_send()
 
 
 def on_device(inputs, other_view, mats, vectors, mixing, partner, segments, cotangent):

time: 145 us -> 145 us (level)
  no operation moved by 1% of the time
where the time goes in v6:
time: 145 us; the launch traced here: 144 us
  Pallas kernels  143 us (99%)
    pallas_call x1, Pallas kernels, on_device(): pl.pallas_call(partial(kernel, names, fused), out_shape=[pltpu.VMEM(s[:-1...  136 us
    pallas_call x1, Pallas kernels, on_device(): pl.pallas_call(widen, out_shape=[jax.ShapeDtypeStruct(mats.shape, f32)] +...  6.82 us

profile of v6, /device:TPU:9, one launch (start us, length us, event | category | flops | bytes accessed | tf_op | source)
XLA Modules:
  0.0 143.6 jit_solution(13833195518044127703)
XLA Ops:
  0.6 135.9 %relay.1 = (bf16[256,768]{1,0:T(8,128)(2,1)S(1)}, bf16[2,32,768]{2,1,0:T(8,128)(2,1)S(1)}, bf16[2,64,768]{2,1,0:T(8,128)(2,1)S(1)}, f32[7,1,768]{2,1,0:T(1,128)S(1)}, bf16[8,768,768]{2,1,0:T(8,128)(2,1)S(1)}) custom-call(bf16[2,32,768]{2,1,0:T(8,128)(2,1)} %refs_0_.1, bf16[2,64,768]{2,1,0:T(8,128)(2,1)} %refs_1_.1, bf16[1,2,768,3072]{3,2,1,0:T(8,128)(2,1)} %refs_2_.1, ...), custom_call_target="tpu_custom_call" | custom-call | tf_op jit(solution)/shard_map/relay/pallas_call | solution.py:1136
  136.5 6.8 %widen.1 = (f32[1,2,768,3072]{3,2,1,0:T(8,128)}, bf16[256,768]{1,0:T(8,128)(2,1)}, bf16[2,32,768]{2,1,0:T(8,128)(2,1)}, bf16[2,64,768]{2,1,0:T(8,128)(2,1)}, f32[7,1,768]{2,1,0:T(1,128)}) custom-call(bf16[8,768,768]{2,1,0:T(8,128)(2,1)S(1)} %get-tuple-element.15.total, bf16[256,768]{1,0:T(8,128)(2,1)S(1)} %get-tuple-element.16.refs_0_, ...), custom_call_target="tpu_custom_call" | custom-call | tf_op jit(solution)/shard_map/widen/pallas_call | solution.py:1150
